TPU v7x, 32 devices: a whole 2x2x4 slice. The times are simulated.
32 devices in a mesh: tab: 4 (over x, core), rep: 8 (over z, y).
Axes of the slice: x: 2, y: 2, z: 4, core: 2. Of those that a mesh axis runs over, the one named last changes fastest.
Arguments:
- d_proj: bfloat16 [8, 512, 4, 256], P('rep', 'tab'), may hold values from -6 to 6
- pooled: bfloat16 [8, 512, 4, 512], P('rep', 'tab'), may hold values from -6 to 6
- proj: bfloat16 [4, 512, 256], replicated, may hold values from -0.25 to 0.25
- bag_rows: int32 [8, 512, 4, 8], P('rep', None, 'tab'), may hold values from 0 to 511
- bag_lengths: int32 [8, 512, 4], P('rep', None, 'tab'), may hold values from 1 to 8
- dim_blocks: int32 [4], replicated, may hold values from 1 to 16
Outputs:
- emb_grad: float32 [4, 512, 512], P('tab')
- proj_grad: float32 [4, 512, 256], P('tab')
All inputs are finite; a program needn't handle non-finite values.
Results may differ from a plain program's by a relative error of at most 0.003.
Values may be sent and summed in bfloat16 or wider, within the bound.
A program may use at most 64 MiB of HBM per device.

v0:
```python
import jax
import jax.numpy as jnp
from jax import lax
from jax.sharding import PartitionSpec as P

ROWS = 512


def body(d_proj, pooled, proj, bag_rows, bag_lengths, dim_blocks):
    widest = proj.shape[1]
    group_rows = bag_rows.shape[1]
    bag_size = bag_rows.shape[3]
    columns = jnp.arange(widest, dtype=jnp.int32)
    live = (columns[None, :] < (widest // 16 * dim_blocks)[:, None]).astype(jnp.float32)
    samples_proj = d_proj[0]
    masked_pool = jnp.where(live[None, :, :] > 0, pooled[0], jnp.zeros_like(pooled[0]))
    proj_part = lax.psum_scatter(
        jnp.einsum("bte,btp->tep", masked_pool, samples_proj, preferred_element_type=jnp.float32),
        "tab",
        scatter_dimension=0,
        tiled=True,
    )
    back = jnp.einsum("btp,tep->bte", samples_proj, proj, preferred_element_type=jnp.float32)
    back = (back * live[None, :, :]).astype(jnp.bfloat16)
    d_pooled = lax.all_to_all(back, "tab", split_axis=1, concat_axis=0, tiled=True)
    row_count = ROWS
    row_ids = jnp.arange(row_count, dtype=jnp.int32)
    counts = jnp.zeros((group_rows, row_count), jnp.float32)
    for slot in range(bag_size):
        hit = (bag_rows[0, :, 0, slot][:, None] == row_ids[None, :]) & (
            slot < bag_lengths[0, :, 0]
        )[:, None]
        counts = counts + hit.astype(jnp.float32)
    grads = [
        lax.dot_general(
            counts.astype(jnp.bfloat16),
            d_pooled[:, 0, :],
            (((0,), (0,)), ((), ())),
            preferred_element_type=jnp.float32,
        )
    ]
    emb_part = jnp.stack(grads, axis=0)
    emb_grad, proj_grad = lax.psum((emb_part, proj_part), "rep")
    return (emb_grad, proj_grad)


def solution(mesh):
    placed = (
        P("rep", "tab", None, None),
        P("rep", "tab", None, None),
        P(),
        P("rep", None, "tab", None),
        P("rep", None, "tab"),
        P(),
    )
    return jax.shard_map(
        body,
        mesh=mesh,
        in_specs=placed,
        out_specs=(P("tab", None, None), P("tab", None, None)),
        check_vma=False,
    )
```

profile of v0, /device:TPU:0, one launch (start us, length us, event | category | flops | bytes accessed | tf_op | source)
XLA Modules:
  0.0 150.4 jit_solution(9416447786491123470)
XLA Ops:
  7.2 0.0 copy-start
  7.2 0.0 reduce-scatter.2.cloned.1.call-start
  7.2 0.7 broadcast_multiply_fusion
  8.0 0.1 broadcast_compare_fusion
  8.0 1.3 bitcast_select_fusion
  9.3 0.0 copy-start.2
  9.3 2.9 %fusion.10 = f32[4,512,256]{2,1,0:T(8,128)} fusion(bf16[128,4,512]{2,1,0:T(4,128)(2,1)S(1)} %bitcast_select_fusion, bf16[128,4,256]{2,1,0:T(4,128)(2,1)} %bitcast.23), kind=kOutput, calls=%fused_computation.22 | convolution fusion | flops 134217728 | bytes 2883584 | tf_op jit(solution)/shard_map/bte,btp->tep/dot_general | solution.py:18
  12.2 0.0 copy-start.4
  12.2 0.0 copy-start.3
  12.2 0.0 reduce-scatter.2.cloned.1.call-update
  12.2 0.0 copy-done
  12.2 0.0 copy-done.2
  12.2 1.2 fusion.1
  13.5 4.2 %all-to-all-start = ((bf16[128,4,512]{0,2,1:T(8,128)(2,1)}), bf16[128,4,512]{0,2,1:T(8,128)(2,1)S(1)}, u32[]{:S(2)}, u32[]{:S(2)}) async-start(bf16[128,4,512]{0,2,1:T(8,128)(2,1)} %fusion.1), calls=%async_computation | async-start | bytes 1048576 | tf_op jit(solution)/shard_map/all_to_all | solution.py:25
  17.7 0.0 all-reduce.3.cloned.1.call-start
  17.7 0.0 copy-done.4
  17.7 0.1 compare_reduce_fusion.7
  17.7 0.0 copy-done.3
  17.8 8.8 %all-to-all-done = bf16[128,4,512]{0,2,1:T(8,128)(2,1)S(1)} async-done(((bf16[128,4,512]{0,2,1:T(8,128)(2,1)}), bf16[128,4,512]{0,2,1:T(8,128)(2,1)S(1)}, u32[]{:S(2)}, u32[]{:S(2)}) %all-to-all-start) | async-done | bytes 524320 | tf_op jit(solution)/shard_map/all_to_all | solution.py:25
  26.5 0.2 copy.12
  26.7 3.1 %convolution_bitcast_fusion = f32[1,512,512]{2,1,0:T(8,128)} fusion(bf16[512,512]{1,0:T(8,128)(2,1)S(1)} %bitcast.22, s32[512]{0:T(512)S(1)} %bitcast.31, s32[512]{0:T(512)S(1)} %bitcast.32, s32[512]{0:T(512)S(1)} %bitcast.26, s32[512]{0:T(512)S(1)} %bitcast.27, s32[512]{0:T(512)S(1)} %bitcast.28, s32[512]{0:T(512)S(1)} %bitcast.29, s32[512]{0:T(512)S(1)} %bitcast.30, ...), kind=kOutput, calls=%fused_computation | convolution fusion | flops 276824064 | bytes 1593344 | tf_op jit(solution)/shard_map/dot_general | solution.py:35
  29.8 16.7 %reduce-scatter.2.cloned.1.call-done = f32[1,512,256]{2,1,0:T(8,128)} async-done(((f32[4,512,256]{2,1,0:T(8,128)}), f32[1,512,256]{2,1,0:T(8,128)}) %reduce-scatter.2.cloned.1.call-update) | async-done | bytes 524304 | tf_op jit(solution)/shard_map/reduce_scatter | solution.py:17
  46.5 0.0 all-reduce.3.cloned.1.call-update
  46.5 93.9 %all-reduce.3.cloned.1.call-done = (f32[1,512,512]{2,1,0:T(8,128)}, f32[1,512,256]{2,1,0:T(8,128)}) async-done(((f32[1,512,512]{2,1,0:T(8,128)}, f32[1,512,256]{2,1,0:T(8,128)}), (f32[1,512,512]{2,1,0:T(8,128)}, f32[1,512,256]{2,1,0:T(8,128)})) %all-reduce.3.cloned.1.call-update) | async-done | bytes 1572880 | tf_op jit(solution)/shard_map/psum | solution.py:43
  140.4 0.0 copy-start.1
  140.4 2.3 %copy.23 = f32[1,512,512]{2,1,0:T(8,128)} copy(f32[1,512,512]{2,1,0:T(8,128)} %get-tuple-element.22) | data formatting | bytes 2097152
  142.8 0.0 copy-done.1
  142.8 0.8 copy.24
  (1 shorter events, 0.0 us)
Async XLA Ops:
  7.2 5.0 %copy-start = (bf16[4,512,256]{2,1,0:T(8,128)(2,1)S(1)}, bf16[4,512,256]{2,1,0:T(8,128)(2,1)}, u32[]{:S(2)}) copy-start(bf16[4,512,256]{2,1,0:T(8,128)(2,1)} %param.8) | copy-start | bytes 3145732
  7.2 39.3 %reduce-scatter.2.cloned.1.call-start = ((), (), s32[]{:S(2)}) async-start(), calls=%async_computation.2 | async-start | bytes 2621440 | tf_op jit(solution)/shard_map/reduce_scatter | solution.py:17
  9.3 2.9 %copy-start.2 = (bf16[1,128,4,256]{3,2,1,0:T(4,128)(2,1)S(1)}, bf16[1,128,4,256]{3,2,1,0:T(4,128)(2,1)}, u32[]{:S(2)}) copy-start(bf16[1,128,4,256]{3,2,1,0:T(4,128)(2,1)} %param.6) | copy-start | bytes 786436
  12.2 5.5 %copy-start.4 = (s32[1,512,1]{1,2,0:T(1,128)S(1)}, s32[1,512,1]{1,2,0:T(1,128)}, u32[]{:S(2)}) copy-start(s32[1,512,1]{1,2,0:T(1,128)} %param.10) | copy-start | bytes 6148
  12.2 5.6 %copy-start.3 = (s32[1,512,1,8]{1,3,2,0:T(8,128)S(1)}, s32[1,512,1,8]{1,3,2,0:T(8,128)}, u32[]{:S(2)}) copy-start(s32[1,512,1,8]{1,3,2,0:T(8,128)} %param.9) | copy-start | bytes 49156
  13.5 13.1 %all-to-all-start = ((bf16[128,4,512]{0,2,1:T(8,128)(2,1)}), bf16[128,4,512]{0,2,1:T(8,128)(2,1)S(1)}, u32[]{:S(2)}, u32[]{:S(2)}) async-start(bf16[128,4,512]{0,2,1:T(8,128)(2,1)} %fusion.1), calls=%async_computation | async-start | bytes 1048576 | tf_op jit(solution)/shard_map/all_to_all | solution.py:25
  17.7 122.8 %all-reduce.3.cloned.1.call-start = ((), (), s32[]{:S(2)}) async-start(), calls=%async_computation.3 | async-start | bytes 3145728 | tf_op jit(solution)/shard_map/psum | solution.py:43
  140.4 2.3 %copy-start.1 = (f32[1,512,256]{2,1,0:T(8,128)S(1)}, f32[1,512,256]{2,1,0:T(8,128)}, u32[]{:S(2)}) copy-start(f32[1,512,256]{2,1,0:T(8,128)} %get-tuple-element.23) | copy-start | bytes 1572868
Sparse Core Ops, SparseCore 0:
  12.3 34.1 reduce-scatter.1
  51.1 89.2 all-reduce.2
where the time goes:
time: 151 us; the launch traced here: 150 us
  waiting for transfers between devices  119 us (79%)
  between operations  14.1 us (9%)
  matrix products  7.19 us (5%)
  starting transfers between devices  4.25 us (3%)
  local copies, waits for them, and re-layouts  3.37 us (2%)
  other arithmetic  2.12 us (1%)
    psum x1, waiting for transfers between devices, body(): emb_grad, proj_grad = lax.psum((emb_part, proj_part), 'rep')  93.9 us
    reduce_scatter x1, waiting for transfers between devices, body(): lax.psum_scatter(jnp.einsum('bte,btp->tep', masked_pool, samples_proj, pr...  16.7 us
    all_to_all x1, waiting for transfers between devices, body(): lax.all_to_all(back, 'tab', split_axis=1, concat_axis=0, tiled=True)  8.75 us
    all_to_all x1, starting transfers between devices, body(): lax.all_to_all(back, 'tab', split_axis=1, concat_axis=0, tiled=True)  4.21 us
    unnamed x12, local copies, waits for them, and re-layouts  3.14 us
    dot_general x1, matrix products, body(): lax.dot_general(counts.astype(jnp.bfloat16), d_pooled[:, 0, :], (((0,), (...  3.09 us
  transfers between devices with their start and end apart: 3, of which 3 were waited for; matrix products, arithmetic and copies ran while one was open for 3% of the time, Pallas kernels for 0%

commit v1 on v0

v1 whole, which is shorter than its diff:
```python
import functools

import jax
import jax.numpy as jnp
from jax import lax
from jax.experimental import pallas as pl
from jax.experimental.pallas import tpu as pltpu
from jax.sharding import PartitionSpec as P

ROWS = 512
MESH = pl.DeviceIdType.MESH
BF16 = jnp.bfloat16
F32 = jnp.float32


def kernel(
    n_tab,
    n_rep,
    dproj_ref,
    pooled_ref,
    rows_ref,
    lens_ref,
    out_row,
    out_proj,
    dproj_all,
    pooled_all,
    counts,
    own_row,
    own_proj,
    send_row,
    send_proj,
    recv_row,
    recv_proj,
    own_sem,
    a_send,
    a_recv,
    s_send,
    s_recv,
    g_send,
    g_recv,
):
    tab = lax.axis_index("tab")
    rep = lax.axis_index("rep")
    n_samples = dproj_ref.shape[1]
    part = out_row.shape[1]
    n_pair = n_rep // 2
    partner = rep + 1 - 2 * lax.rem(rep, 2)

    def remote(src, dst, send, recv, tab_to, rep_to):
        return pltpu.make_async_remote_copy(
            src_ref=src,
            dst_ref=dst,
            send_sem=send,
            recv_sem=recv,
            device_id=(tab_to, rep_to),
            device_id_type=MESH,
        )

    barrier = pltpu.get_barrier_semaphore()
    for k in range(1, n_tab):
        pl.semaphore_signal(
            barrier, inc=1, device_id=(lax.rem(tab + k, n_tab), rep), device_id_type=MESH
        )
    for k in range(1, n_rep):
        pl.semaphore_signal(
            barrier, inc=1, device_id=(tab, lax.rem(rep + k, n_rep)), device_id_type=MESH
        )
    pl.semaphore_wait(barrier, n_tab + n_rep - 2)

    gathers = []
    for which, (src, dst) in enumerate(((dproj_ref, dproj_all), (pooled_ref, pooled_all))):
        copies = []
        for k in range(1, n_tab):
            to = lax.rem(tab + k, n_tab)
            copy = remote(
                src.at[to], dst.at[tab], a_send.at[which, k], a_recv.at[which, k], to, rep
            )
            copy.start()
            copies.append(copy)
        gathers.append(copies)
    own = [
        pltpu.make_async_copy(src.at[tab], dst.at[tab], own_sem.at[which])
        for which, (src, dst) in enumerate(((dproj_ref, dproj_all), (pooled_ref, pooled_all)))
    ]
    for copy in own:
        copy.start()

    named = rows_ref[...]
    slots = lax.broadcasted_iota(jnp.int32, named.shape, 0)
    named = jnp.where(slots < lens_ref[...], named, -1)
    step = 64

    def count(i, carry):
        at = pl.multiple_of(i * step, step)
        ids = lax.broadcasted_iota(jnp.int32, (step, named.shape[1]), 0) + at
        total = jnp.zeros((step, named.shape[1]), F32)
        for slot in range(named.shape[0]):
            total = total + jnp.where(named[slot : slot + 1, :] == ids, 1.0, 0.0)
        counts[pl.ds(at, step), :] = total.astype(BF16)
        return carry

    lax.fori_loop(0, counts.shape[0] // step, count, 0)

    def scatter(which, partial, own_sum, send, recv):
        own_sum[...] = partial.reshape(own_sum.shape)
        send[...] = partial.reshape(own_sum.shape).astype(BF16)
        copies = []
        for k in range(1, n_rep):
            to = lax.rem(rep + k, n_rep)
            copy = remote(
                send.at[to], recv.at[k], s_send.at[which, k], s_recv.at[which, k], tab, to
            )
            copy.start()
            copies.append(copy)
        return copies

    own[0].wait()
    for copy in gathers[0]:
        copy.wait_recv()
    d_all = dproj_all[...].reshape(n_tab * n_samples, -1)
    row_part = jnp.dot(counts[...], d_all, preferred_element_type=F32)
    row_copies = scatter(0, row_part, own_row, send_row, recv_row)

    own[1].wait()
    for copy in gathers[1]:
        copy.wait_recv()
    p_all = pooled_all[...].reshape(n_tab * n_samples, -1)
    proj_part = lax.dot_general(
        p_all, dproj_all[...].reshape(n_tab * n_samples, -1), (((0,), (0,)), ((), ())),
        preferred_element_type=F32,
    )
    proj_copies = scatter(1, proj_part, own_proj, send_proj, recv_proj)

    def reduce(which, copies, own_sum, recv, out):
        for copy in copies:
            copy.wait_recv()
        total = own_sum[rep]
        for k in range(1, n_rep):
            total = total + recv[k].astype(F32)
        out[rep] = total.astype(BF16)
        started = []
        for k in range(1, n_pair):
            copy = remote(
                out.at[rep], out.at[rep], g_send.at[which, 0, k], g_recv.at[which, 0, k],
                tab, lax.rem(rep + 2 * k, n_rep),
            )
            copy.start()
            started.append(copy)
        pair = remote(
            out.at[rep], out.at[rep], g_send.at[which, 1, 0], g_recv.at[which, 1, 0], tab, partner
        )
        pair.start()
        return started, pair

    def forward(which, started, out):
        copies = []
        for k in range(1, n_pair):
            started[k - 1].wait_recv()
            origin = lax.rem(rep - 2 * k + n_rep, n_rep)
            copy = remote(
                out.at[origin], out.at[origin], g_send.at[which, 1, k], g_recv.at[which, 1, k],
                tab, partner,
            )
            copy.start()
            copies.append(copy)
        return copies

    row_out, row_pair = reduce(0, row_copies, own_row, recv_row, out_row)
    proj_out, proj_pair = reduce(1, proj_copies, own_proj, recv_proj, out_proj)
    row_fwd = forward(0, row_out, out_row)
    proj_fwd = forward(1, proj_out, out_proj)
    for copy in [row_pair, *row_fwd, proj_pair, *proj_fwd]:
        copy.wait()
    for copy in [*gathers[0], *gathers[1], *row_copies, *proj_copies, *row_out, *proj_out]:
        copy.wait_send()


def fused(n_tab, n_rep, d_proj, pooled, proj, bag_rows, bag_lengths, dim_blocks):
    n_samples, width, widest = d_proj.shape[1], d_proj.shape[3], pooled.shape[3]
    group, bag = bag_rows.shape[1], bag_rows.shape[3]
    part, proj_part = ROWS // n_rep, widest // n_rep
    by_table = jnp.transpose(d_proj[0], (1, 0, 2))
    pooled_by_table = jnp.transpose(pooled[0], (1, 0, 2))
    vmem = pl.BlockSpec(memory_space=pltpu.VMEM)
    row_sum, proj_sum = pl.pallas_call(
        functools.partial(kernel, n_tab, n_rep),
        out_shape=(
            jax.ShapeDtypeStruct((n_rep, part, width), BF16),
            jax.ShapeDtypeStruct((n_rep, proj_part, width), BF16),
        ),
        in_specs=[vmem] * 4,
        out_specs=(vmem, vmem),
        scratch_shapes=[
            pltpu.VMEM((n_tab, n_samples, width), BF16),
            pltpu.VMEM((n_tab, n_samples, widest), BF16),
            pltpu.VMEM((ROWS, group), BF16),
            pltpu.VMEM((n_rep, part, width), F32),
            pltpu.VMEM((n_rep, proj_part, width), F32),
            pltpu.VMEM((n_rep, part, width), BF16),
            pltpu.VMEM((n_rep, proj_part, width), BF16),
            pltpu.VMEM((n_rep, part, width), BF16),
            pltpu.VMEM((n_rep, proj_part, width), BF16),
            pltpu.SemaphoreType.DMA((2,)),
            pltpu.SemaphoreType.DMA((2, n_tab)),
            pltpu.SemaphoreType.DMA((2, n_tab)),
            pltpu.SemaphoreType.DMA((2, n_rep)),
            pltpu.SemaphoreType.DMA((2, n_rep)),
            pltpu.SemaphoreType.DMA((2, 2, n_rep // 2)),
            pltpu.SemaphoreType.DMA((2, 2, n_rep // 2)),
        ],
        compiler_params=pltpu.CompilerParams(
            collective_id=0, has_side_effects=True, vmem_limit_bytes=32 << 20
        ),
    )(
        by_table,
        pooled_by_table,
        jnp.transpose(bag_rows[0, :, 0, :]),
        bag_lengths.reshape(1, group),
    )
    tab = lax.axis_index("tab")
    live = jnp.arange(widest, dtype=jnp.int32) < widest // 16 * dim_blocks[tab]
    weight = lax.dynamic_index_in_dim(proj, tab, 0, keepdims=False)
    emb = lax.dot_general(
        row_sum.reshape(ROWS, width), weight, (((1,), (1,)), ((), ())),
        preferred_element_type=F32,
    )
    emb = jnp.where(live[None, :], emb, 0.0)
    proj_grad = jnp.where(live[:, None], proj_sum.reshape(widest, width).astype(F32), 0.0)
    return emb[None], proj_grad[None]


def general(d_proj, pooled, proj, bag_rows, bag_lengths, dim_blocks):
    widest = proj.shape[1]
    group_rows = bag_rows.shape[1]
    bag_size = bag_rows.shape[3]
    columns = jnp.arange(widest, dtype=jnp.int32)
    live = (columns[None, :] < (widest // 16 * dim_blocks)[:, None]).astype(F32)
    samples_proj = d_proj[0]
    masked_pool = jnp.where(live[None, :, :] > 0, pooled[0], jnp.zeros_like(pooled[0]))
    proj_part = lax.psum_scatter(
        jnp.einsum("bte,btp->tep", masked_pool, samples_proj, preferred_element_type=F32),
        "tab",
        scatter_dimension=0,
        tiled=True,
    )
    back = jnp.einsum("btp,tep->bte", samples_proj, proj, preferred_element_type=F32)
    back = (back * live[None, :, :]).astype(BF16)
    d_pooled = lax.all_to_all(back, "tab", split_axis=1, concat_axis=0, tiled=True)
    row_ids = jnp.arange(ROWS, dtype=jnp.int32)
    counts = jnp.zeros((group_rows, ROWS), F32)
    for slot in range(bag_size):
        hit = (bag_rows[0, :, 0, slot][:, None] == row_ids[None, :]) & (
            slot < bag_lengths[0, :, 0]
        )[:, None]
        counts = counts + hit.astype(F32)
    emb_part = lax.dot_general(
        counts.astype(BF16), d_pooled[:, 0, :], (((0,), (0,)), ((), ())),
        preferred_element_type=F32,
    )
    return lax.psum((emb_part[None], proj_part), "rep")


def solution(mesh):
    n_tab, n_rep = mesh.shape["tab"], mesh.shape["rep"]
    placed = (
        P("rep", "tab", None, None),
        P("rep", "tab", None, None),
        P(),
        P("rep", None, "tab", None),
        P("rep", None, "tab"),
        P(),
    )

    def body(*args):
        if n_rep % 2 == 0 and ROWS % (16 * n_rep) == 0 and args[2].shape[1] % (16 * n_rep) == 0:
            return fused(n_tab, n_rep, *args)
        return general(*args)

    return jax.shard_map(
        body,
        mesh=mesh,
        in_specs=placed,
        out_specs=(P("tab", None, None), P("tab", None, None)),
        check_vma=False,
    )
```

time: 151 us -> 42.2 us (0.28)
  waiting for transfers between devices: 119 us -> 0 us
  Pallas kernels: 0 us -> 35.1 us
  between operations: 14.1 us -> 1.37 us
  matrix products: 7.19 us -> 1.31 us
  starting transfers between devices: 4.25 us -> 0 us
    psum x1 -> x0, waiting for transfers between devices: 93.9 us -> none  [body(): emb_grad, proj_grad = lax.psum((emb_part, proj_part), 'rep')]
    pallas_call x0 -> x1, Pallas kernels: none -> 35.1 us  [fused(): pl.pallas_call(functools.partial(kernel, n_tab, n_rep), out_shape=(jax.Sh...]
    reduce_scatter x1 -> x0, waiting for transfers between devices: 16.7 us -> none  [body(): lax.psum_scatter(jnp.einsum('bte,btp->tep', masked_pool, samples_proj, pr...]
    all_to_all x1 -> x0, waiting for transfers between devices: 8.75 us -> none  [body(): lax.all_to_all(back, 'tab', split_axis=1, concat_axis=0, tiled=True)]
    dot_general x3 -> x1, matrix products: 7.19 us -> 1.31 us  [fused(): lax.dot_general(row_sum.reshape(ROWS, width), weight, (((1,), (1,)), ((),...]
    all_to_all x1 -> x0, starting transfers between devices: 4.21 us -> none  [body(): lax.all_to_all(back, 'tab', split_axis=1, concat_axis=0, tiled=True)]
  transfers between devices with their start and end apart: 3 -> 0, of which waited for: 3 -> 0; matrix products, arithmetic and copies ran while one was open for 3% -> 0% of each run, Pallas kernels for 0% -> 0%
where the time goes in v1:
time: 42.2 us; the launch traced here: 41.9 us
  Pallas kernels  35.1 us (83%)
  local copies, waits for them, and re-layouts  3.22 us (8%)
  between operations  1.37 us (3%)
  matrix products  1.31 us (3%)
  other arithmetic  0.93 us (2%)
    pallas_call x1, Pallas kernels, fused(): pl.pallas_call(functools.partial(kernel, n_tab, n_rep), out_shape=(jax.Sh...  35.1 us
    unnamed x12, local copies, waits for them, and re-layouts  2.64 us
    dot_general x1, matrix products, fused(): lax.dot_general(row_sum.reshape(ROWS, width), weight, (((1,), (1,)), ((),...  1.31 us
    select_n x1, other arithmetic, fused(): jnp.where(live[:, None], proj_sum.reshape(widest, width).astype(F32), 0.0)  0.93 us

profile of v1, /device:TPU:0, one launch (start us, length us, event | category | flops | bytes accessed | tf_op | source)
XLA Modules:
  0.0 41.9 jit_solution(1827493755322973646)
XLA Ops:
  0.6 0.0 copy-start
  0.6 0.0 copy-start.4
  0.7 0.7 %copy-done.4 = s32[4]{0:T(128)S(1)} copy-done((s32[4]{0:T(128)S(1)}, s32[4]{0:T(128)}, u32[]{:S(2)}) %copy-start.4) | copy-done | bytes 40
  1.4 0.6 %dynamic_slice.7 = s32[1]{0:T(128)} dynamic-slice(s32[4]{0:T(128)S(1)} %copy-done.4, s32[]{:T(128)S(6)} %select_n.20), dynamic_slice_sizes={1} | dynamic-slice | bytes 12 | tf_op jit(solution)/shard_map/dynamic_slice | solution.py:221
  2.6 0.0 copy-start.3
  2.7 1.2 %copy.12 = bf16[1,128,4,512]{3,1,2,0:T(8,128)(2,1)S(1)} copy(bf16[1,128,4,512]{3,2,1,0:T(4,128)(2,1)} %param.7) | data formatting | bytes 1048576 | tf_op args[1]
  3.8 0.0 copy-done.3
  3.8 0.0 copy-start.1
  3.9 0.0 copy-start.2
  3.9 0.7 %copy-done.1 = s32[1,512,1,8]{1,3,2,0:T(8,128)S(1)} copy-done((s32[1,512,1,8]{1,3,2,0:T(8,128)S(1)}, s32[1,512,1,8]{1,3,2,0:T(8,128)}, u32[]{:S(2)}) %copy-start.1) | copy-done | bytes 16408
  4.6 0.0 copy-done.2
  4.6 35.1 %shard_map.77 = (bf16[8,64,256]{2,1,0:T(8,128)(2,1)S(1)}, bf16[8,64,256]{2,1,0:T(8,128)(2,1)S(1)}) custom-call(bf16[4,128,256]{2,1,0:T(8,128)(2,1)S(1)} %bitcast.27, bf16[4,128,512]{2,1,0:T(8,128)(2,1)S(1)} %bitcast.26, s32[8,512]{1,0:T(8,128)S(1)} %bitcast.30, s32[1,512]{1,0:T(1,128)S(1)} %bitcast.31), custom_call_target="tpu_custom_call" | custom-call | tf_op jit(solution)/shard_map/pallas_call | solution.py:185
  39.7 0.0 copy-done
  39.7 1.3 %fusion = f32[1,512,512]{2,1,0:T(8,128)} fusion(bf16[512,256]{1,0:T(8,128)(2,1)S(1)} %bitcast.29, pred[512]{0:T(512)(128)(4,1)S(1)} %iota_compare_fusion, bf16[4,512,256]{2,1,0:T(8,128)(2,1)S(1)} %copy-done, s32[]{:T(128)S(6)} %select_n.20), kind=kOutput, calls=%fused_computation.1 | convolution fusion | flops 134479872 | bytes 1573380 | tf_op jit(solution)/shard_map/dot_general | solution.py:223
  41.0 0.9 %convert_select_fusion = f32[1,512,256]{2,1,0:T(8,128)} fusion(pred[512]{0:T(512)(128)(4,1)S(1)} %iota_compare_fusion, bf16[1,512,256]{2,1,0:T(8,128)(2,1)S(1)} %bitcast.28), kind=kLoop, calls=%fused_computation.2 | loop fusion | flops 262144 | bytes 786944 | tf_op jit(solution)/shard_map/jit(_where)/select_n | solution.py:228
  (2 shorter events, 0.0 us)
Async XLA Ops:
  0.6 39.1 %copy-start = (bf16[4,512,256]{2,1,0:T(8,128)(2,1)S(1)}, bf16[4,512,256]{2,1,0:T(8,128)(2,1)}, u32[]{:S(2)}) copy-start(bf16[4,512,256]{2,1,0:T(8,128)(2,1)} %param.8) | copy-start | bytes 3145732
  0.6 0.7 %copy-start.4 = (s32[4]{0:T(128)S(1)}, s32[4]{0:T(128)}, u32[]{:S(2)}) copy-start(s32[4]{0:T(128)} %param.11) | copy-start | bytes 52
  2.6 1.2 %copy-start.3 = (bf16[1,128,4,256]{3,2,1,0:T(4,128)(2,1)S(1)}, bf16[1,128,4,256]{3,2,1,0:T(4,128)(2,1)}, u32[]{:S(2)}) copy-start(bf16[1,128,4,256]{3,2,1,0:T(4,128)(2,1)} %param.6) | copy-start | bytes 786436
  3.8 0.7 %copy-start.1 = (s32[1,512,1,8]{1,3,2,0:T(8,128)S(1)}, s32[1,512,1,8]{1,3,2,0:T(8,128)}, u32[]{:S(2)}) copy-start(s32[1,512,1,8]{1,3,2,0:T(8,128)} %param.9) | copy-start | bytes 49156
  3.9 0.7 %copy-start.2 = (s32[1,512,1]{1,2,0:T(1,128)S(1)}, s32[1,512,1]{1,2,0:T(1,128)}, u32[]{:S(2)}) copy-start(s32[1,512,1]{1,2,0:T(1,128)} %param.10) | copy-start | bytes 6148

commit v2 on v1

v2 whole, which is shorter than its diff:
```python
import functools

import jax
import jax.numpy as jnp
from jax import lax
from jax.experimental import pallas as pl
from jax.experimental.pallas import tpu as pltpu
from jax.sharding import PartitionSpec as P

ROWS = 512
MESH = pl.DeviceIdType.MESH
BF16 = jnp.bfloat16
F32 = jnp.float32


def kernel(
    n_tab,
    n_rep,
    dproj_ref,
    pooled_ref,
    rows_hbm,
    lens_hbm,
    out_row,
    out_proj,
    rows_ref,
    lens_ref,
    dproj_all,
    pooled_all,
    counts,
    row_own,
    row_wire,
    proj_own,
    proj_wire,
    own_sem,
    a_send,
    a_recv,
    y_send,
    y_recv,
    z_send,
    z_recv,
    g_send,
    g_recv,
):
    tab = lax.axis_index("tab")
    rep = lax.axis_index("rep")
    n_z = n_rep // 2
    y = lax.rem(rep, 2)
    z = rep // 2
    partner = rep + 1 - 2 * y
    n_samples, width = dproj_ref.shape[1], dproj_ref.shape[2]
    piece = pooled_ref.shape[2] // 2

    def remote(src, dst, send, recv, tab_to, rep_to):
        return pltpu.make_async_remote_copy(
            src_ref=src,
            dst_ref=dst,
            send_sem=send,
            recv_sem=recv,
            device_id=(tab_to, rep_to),
            device_id_type=MESH,
        )

    barrier = pltpu.get_barrier_semaphore()
    for k in range(1, n_tab):
        pl.semaphore_signal(
            barrier, inc=1, device_id=(lax.rem(tab + k, n_tab), rep), device_id_type=MESH
        )
    for k in range(1, n_z):
        pl.semaphore_signal(
            barrier, inc=1, device_id=(tab, lax.rem(rep + 2 * k, n_rep)), device_id_type=MESH
        )
    pl.semaphore_signal(barrier, inc=1, device_id=(tab, partner), device_id_type=MESH)
    bags = [
        pltpu.make_async_copy(rows_hbm, rows_ref, own_sem.at[2]),
        pltpu.make_async_copy(lens_hbm, lens_ref, own_sem.at[3]),
    ]
    for copy in bags:
        copy.start()
    pl.semaphore_wait(barrier, n_tab - 1 + n_z)

    def columns(ref, at, which):
        return ref.at[at] if which == 0 else ref.at[at, :, pl.ds((which - 1) * piece, piece)]

    gathers = []
    for which in range(3):
        src, dst = (dproj_ref, dproj_all) if which == 0 else (pooled_ref, pooled_all)
        copies = []
        for k in range(1, n_tab):
            to = lax.rem(tab + k, n_tab)
            copy = remote(
                columns(src, to, which), columns(dst, tab, which),
                a_send.at[which, k], a_recv.at[which, k], to, rep,
            )
            copy.start()
            copies.append(copy)
        gathers.append(copies)
    own = [
        pltpu.make_async_copy(src.at[tab], dst.at[tab], own_sem.at[which])
        for which, (src, dst) in enumerate(((dproj_ref, dproj_all), (pooled_ref, pooled_all)))
    ]
    for copy in own:
        copy.start()

    for copy in bags:
        copy.wait()
    named = rows_ref[...]
    slots = lax.broadcasted_iota(jnp.int32, named.shape, 0)
    named = jnp.where(slots < lens_ref[...], named, -1)
    step = 64

    def count(i, carry):
        at = pl.multiple_of(i * step, step)
        ids = lax.broadcasted_iota(jnp.int32, (step, named.shape[1]), 0) + at
        total = jnp.zeros((step, named.shape[1]), F32)
        for slot in range(named.shape[0]):
            total = total + jnp.where(named[slot : slot + 1, :] == ids, 1.0, 0.0)
        counts[pl.ds(at, step), :] = total.astype(BF16)
        return carry

    lax.fori_loop(0, counts.shape[0] // step, count, 0)

    buffers = [
        (row_own, row_wire, out_row),
        (proj_own.at[0], proj_wire.at[0], out_proj.at[0]),
        (proj_own.at[1], proj_wire.at[1], out_proj.at[1]),
    ]

    def send_pair(which):
        sums, wire, _ = buffers[which]
        wire[0] = sums[1 - y].astype(BF16)
        copy = remote(wire.at[0], wire.at[1], y_send.at[which], y_recv.at[which], tab, partner)
        copy.start()
        return copy

    def send_line(which, pair):
        sums, wire, _ = buffers[which]
        pair.wait_recv()
        total = sums[y] + wire[1].astype(F32)
        wire[2] = total.astype(BF16)
        copies = []
        for k in range(1, n_z):
            to = lax.rem(z + k, n_z)
            copy = remote(
                wire.at[2, to], wire.at[3, k], z_send.at[which, k], z_recv.at[which, k],
                tab, 2 * to + y,
            )
            copy.start()
            copies.append(copy)
        sums[y] = total
        return copies

    def send_sums(which, line):
        sums, wire, out = buffers[which]
        for copy in line:
            copy.wait_recv()
        total = sums[y, z]
        for k in range(1, n_z):
            total = total + wire[3, k].astype(F32)
        high = total.astype(BF16)
        if which == 0:
            out[y, z, :, :width] = high
            out[y, z, :, width:] = (total - high.astype(F32)).astype(BF16)
        else:
            out[y, z] = high
        block = out.at[y, z]
        copies = []
        for k in range(1, n_z):
            copy = remote(
                block, block, g_send.at[which, 0, k], g_recv.at[which, 0, k],
                tab, 2 * lax.rem(z + k, n_z) + y,
            )
            copy.start()
            copies.append(copy)
        copy = remote(
            block, block, g_send.at[which, 1, 0], g_recv.at[which, 1, 0], tab, partner
        )
        copy.start()
        return copies, copy

    def forward(which, arriving):
        out = buffers[which][2]
        copies = []
        for k in range(1, n_z):
            arriving[k - 1].wait_recv()
            block = out.at[y, lax.rem(z - k + n_z, n_z)]
            copy = remote(
                block, block, g_send.at[which, 1, k], g_recv.at[which, 1, k], tab, partner
            )
            copy.start()
            copies.append(copy)
        return copies

    def project(half):
        total = None
        for k in range(n_tab):
            if k > 0:
                gathers[1 + half][k - 1].wait_recv()
            at = lax.rem(tab - k + n_tab, n_tab)
            term = lax.dot_general(
                pooled_all[at, :, half * piece : (half + 1) * piece], dproj_all[at],
                (((0,), (0,)), ((), ())), preferred_element_type=F32,
            )
            total = term if total is None else total + term
        proj_own[half] = total.reshape(proj_own.shape[1:])
        return send_pair(1 + half)

    own[0].wait()
    for copy in gathers[0]:
        copy.wait_recv()
    d_all = dproj_all[...].reshape(n_tab * n_samples, width)
    row_own[...] = jnp.dot(counts[...], d_all, preferred_element_type=F32).reshape(row_own.shape)
    pair0 = send_pair(0)
    own[1].wait()
    pair1 = project(0)
    line0 = send_line(0, pair0)
    pair2 = project(1)
    line1 = send_line(1, pair1)
    line2 = send_line(2, pair2)
    sums0, last0 = send_sums(0, line0)
    sums1, last1 = send_sums(1, line1)
    sums2, last2 = send_sums(2, line2)
    fwd0 = forward(0, sums0)
    fwd1 = forward(1, sums1)
    fwd2 = forward(2, sums2)
    for copy in [last0, *fwd0, last1, *fwd1, last2, *fwd2]:
        copy.wait()
    for copy in [
        *gathers[0], *gathers[1], *gathers[2], pair0, pair1, pair2,
        *line0, *line1, *line2, *sums0, *sums1, *sums2,
    ]:
        copy.wait_send()


def finish(dims_ref, row_ref, sum_ref, weight_ref, emb_ref, proj_ref):
    tab = lax.axis_index("tab")
    widest = weight_ref.shape[1]
    limit = widest // 16 * dims_ref[tab]
    weight = weight_ref[tab]
    width = weight.shape[1]
    rows = row_ref[...]
    emb = lax.dot_general(
        rows[:, :width], weight, (((1,), (1,)), ((), ())), preferred_element_type=F32
    ) + lax.dot_general(
        rows[:, width:], weight, (((1,), (1,)), ((), ())), preferred_element_type=F32
    )
    emb_ref[0] = jnp.where(lax.broadcasted_iota(jnp.int32, emb.shape, 1) < limit, emb, 0.0)
    total = sum_ref[...].astype(F32)
    at = lax.broadcasted_iota(jnp.int32, total.shape, 0) + pl.program_id(0) * total.shape[0]
    proj_ref[0] = jnp.where(at < limit, total, 0.0)


def fused(n_tab, n_rep, d_proj, pooled, proj, bag_rows, bag_lengths, dim_blocks):
    n_samples, width, widest = d_proj.shape[1], d_proj.shape[3], pooled.shape[3]
    group, bag = bag_rows.shape[1], bag_rows.shape[3]
    n_z = n_rep // 2
    part, proj_part = ROWS // n_rep, widest // 2 // n_rep
    by_table = jnp.transpose(d_proj[0], (1, 0, 2))
    pooled_by_table = jnp.transpose(pooled[0], (1, 0, 2))
    vmem = pl.BlockSpec(memory_space=pltpu.VMEM)
    hbm = pl.BlockSpec(memory_space=pl.ANY)
    dma = pltpu.SemaphoreType.DMA
    row_sum, proj_sum = pl.pallas_call(
        functools.partial(kernel, n_tab, n_rep),
        out_shape=(
            jax.ShapeDtypeStruct((2, n_z, part, 2 * width), BF16),
            jax.ShapeDtypeStruct((2, 2, n_z, proj_part, width), BF16),
        ),
        in_specs=[vmem, vmem, hbm, hbm],
        out_specs=(vmem, vmem),
        scratch_shapes=[
            pltpu.VMEM((bag, group), jnp.int32),
            pltpu.VMEM((1, group), jnp.int32),
            pltpu.VMEM((n_tab, n_samples, width), BF16),
            pltpu.VMEM((n_tab, n_samples, widest), BF16),
            pltpu.VMEM((ROWS, group), BF16),
            pltpu.VMEM((2, n_z, part, width), F32),
            pltpu.VMEM((4, n_z, part, width), BF16),
            pltpu.VMEM((2, 2, n_z, proj_part, width), F32),
            pltpu.VMEM((2, 4, n_z, proj_part, width), BF16),
            dma((4,)),
            dma((3, n_tab)),
            dma((3, n_tab)),
            dma((3,)),
            dma((3,)),
            dma((3, n_z)),
            dma((3, n_z)),
            dma((3, 2, n_z)),
            dma((3, 2, n_z)),
        ],
        compiler_params=pltpu.CompilerParams(
            collective_id=0, has_side_effects=True, vmem_limit_bytes=32 << 20
        ),
    )(
        by_table,
        pooled_by_table,
        jnp.transpose(bag_rows[0, :, 0, :]),
        bag_lengths.reshape(1, group),
    )
    tiles = 4
    emb, proj_grad = pl.pallas_call(
        finish,
        grid=(tiles,),
        out_shape=(
            jax.ShapeDtypeStruct((1, ROWS, widest), F32),
            jax.ShapeDtypeStruct((1, widest, width), F32),
        ),
        in_specs=[
            pl.BlockSpec(memory_space=pltpu.SMEM),
            pl.BlockSpec((ROWS // tiles, 2 * width), lambda i: (i, 0)),
            pl.BlockSpec((widest // tiles, width), lambda i: (i, 0)),
            vmem,
        ],
        out_specs=(
            pl.BlockSpec((1, ROWS // tiles, widest), lambda i: (0, i, 0)),
            pl.BlockSpec((1, widest // tiles, width), lambda i: (0, i, 0)),
        ),
        compiler_params=pltpu.CompilerParams(vmem_limit_bytes=16 << 20),
        cost_estimate=pl.CostEstimate(
            flops=4 * ROWS * widest * width,
            bytes_accessed=4 * ROWS * widest + 6 * widest * width,
            transcendentals=0,
        ),
    )(dim_blocks, row_sum.reshape(ROWS, 2 * width), proj_sum.reshape(widest, width), proj)
    return emb, proj_grad


def general(d_proj, pooled, proj, bag_rows, bag_lengths, dim_blocks):
    widest = proj.shape[1]
    group_rows = bag_rows.shape[1]
    bag_size = bag_rows.shape[3]
    columns = jnp.arange(widest, dtype=jnp.int32)
    live = (columns[None, :] < (widest // 16 * dim_blocks)[:, None]).astype(F32)
    samples_proj = d_proj[0]
    masked_pool = jnp.where(live[None, :, :] > 0, pooled[0], jnp.zeros_like(pooled[0]))
    proj_part = lax.psum_scatter(
        jnp.einsum("bte,btp->tep", masked_pool, samples_proj, preferred_element_type=F32),
        "tab",
        scatter_dimension=0,
        tiled=True,
    )
    back = jnp.einsum("btp,tep->bte", samples_proj, proj, preferred_element_type=F32)
    back = (back * live[None, :, :]).astype(BF16)
    d_pooled = lax.all_to_all(back, "tab", split_axis=1, concat_axis=0, tiled=True)
    row_ids = jnp.arange(ROWS, dtype=jnp.int32)
    counts = jnp.zeros((group_rows, ROWS), F32)
    for slot in range(bag_size):
        hit = (bag_rows[0, :, 0, slot][:, None] == row_ids[None, :]) & (
            slot < bag_lengths[0, :, 0]
        )[:, None]
        counts = counts + hit.astype(F32)
    emb_part = lax.dot_general(
        counts.astype(BF16), d_pooled[:, 0, :], (((0,), (0,)), ((), ())),
        preferred_element_type=F32,
    )
    return lax.psum((emb_part[None], proj_part), "rep")


def solution(mesh):
    n_tab, n_rep = mesh.shape["tab"], mesh.shape["rep"]
    placed = (
        P("rep", "tab", None, None),
        P("rep", "tab", None, None),
        P(),
        P("rep", None, "tab", None),
        P("rep", None, "tab"),
        P(),
    )

    def body(*args):
        if n_rep % 2 == 0 and ROWS % (16 * n_rep) == 0 and args[2].shape[1] % (32 * n_rep) == 0:
            return fused(n_tab, n_rep, *args)
        return general(*args)

    return jax.shard_map(
        body,
        mesh=mesh,
        in_specs=placed,
        out_specs=(P("tab", None, None), P("tab", None, None)),
        check_vma=False,
    )
```

time: 42.2 us -> 41.7 us (0.988)
  Pallas kernels: 35.1 us -> 38 us
  matrix products: 1.31 us -> 0 us
  other arithmetic: 0.93 us -> 0 us
  between operations: 1.37 us -> 0.7 us
    pallas_call x0 -> x1, Pallas kernels: none -> 2.93 us  [fused(): pl.pallas_call(finish, grid=(tiles,), out_shape=(jax.ShapeDtypeStruct((1,...]
    dot_general x1 -> x0, matrix products: 1.31 us -> none  [fused(): lax.dot_general(row_sum.reshape(ROWS, width), weight, (((1,), (1,)), ((),...]
    select_n x1 -> x0, other arithmetic: 0.93 us -> none  [fused(): jnp.where(live[:, None], proj_sum.reshape(widest, width).astype(F32), 0.0)]
    dynamic_slice x1 -> x0, local copies, waits for them, and re-layouts: 0.58 us -> none  [fused(): live = jnp.arange(widest, dtype=jnp.int32) < widest // 16 * dim_blocks[tab]]
    unnamed x12 -> x10, local copies, waits for them, and re-layouts: 2.64 us -> 2.87 us
where the time goes in v2:
time: 41.7 us; the launch traced here: 41.5 us
  Pallas kernels  38 us (91%)
  local copies, waits for them, and re-layouts  2.87 us (7%)
  between operations  0.7 us (2%)
    pallas_call x1, Pallas kernels, fused(): pl.pallas_call(functools.partial(kernel, n_tab, n_rep), out_shape=(jax.Sh...  35 us
    pallas_call x1, Pallas kernels, fused(): pl.pallas_call(finish, grid=(tiles,), out_shape=(jax.ShapeDtypeStruct((1,...  2.93 us
    unnamed x10, local copies, waits for them, and re-layouts  2.87 us

profile of v2, /device:TPU:0, one launch (start us, length us, event | category | flops | bytes accessed | tf_op | source)
XLA Modules:
  0.0 41.5 jit_solution(2463230942131113179)
XLA Ops:
  0.6 0.0 copy-start.1
  0.6 1.0 %copy.13 = bf16[1,128,4,256]{3,1,2,0:T(8,128)(2,1)S(1)} copy(bf16[1,128,4,256]{3,2,1,0:T(4,128)(2,1)} %param.6) | data formatting | bytes 524288 | tf_op args[0]
  1.6 0.0 copy-start
  1.6 0.0 copy-start.2
  1.7 1.2 %copy.12 = bf16[1,128,4,512]{3,1,2,0:T(8,128)(2,1)S(1)} copy(bf16[1,128,4,512]{3,2,1,0:T(4,128)(2,1)} %param.7) | data formatting | bytes 1048576 | tf_op args[1]
  2.9 0.0 copy-done.1
  2.9 0.0 copy-done.2
  2.9 35.0 %shard_map.77 = (bf16[2,4,64,512]{3,2,1,0:T(8,128)(2,1)S(1)}, bf16[2,2,4,32,256]{4,3,2,1,0:T(8,128)(2,1)S(1)}) custom-call(bf16[4,128,256]{2,1,0:T(8,128)(2,1)S(1)} %bitcast.17, bf16[4,128,512]{2,1,0:T(8,128)(2,1)S(1)} %bitcast.16, s32[8,512]{1,0:T(8,128)S(1)} %bitcast.20, s32[1,512]{1,0:T(1,128)S(1)} %bitcast.21), custom_call_target="tpu_custom_call" | custom-call | tf_op jit(solution)/shard_map/pallas_call | solution.py:262
  37.9 0.0 copy-start.3
  38.0 0.0 copy-done
  38.0 0.6 %copy-done.3 = s32[4]{0:T(128)S(1)} copy-done((s32[4]{0:T(128)S(1)}, s32[4]{0:T(128)}, u32[]{:S(2)}) %copy-start.3) | copy-done | bytes 40
  38.6 2.9 %shard_map.78 = (f32[1,512,512]{2,1,0:T(8,128)}, f32[1,512,256]{2,1,0:T(8,128)}) custom-call(s32[4]{0:T(128)S(1)} %copy-done.3, bf16[512,512]{1,0:T(8,128)(2,1)S(1)} %bitcast.18, bf16[512,256]{1,0:T(8,128)(2,1)S(1)} %bitcast.19, bf16[4,512,256]{2,1,0:T(8,128)(2,1)S(1)} %copy-done), custom_call_target="tpu_custom_call" | custom-call | flops 268435456 | bytes 1835008 | tf_op jit(solution)/shard_map/pallas_call | solution.py:300
Async XLA Ops:
  0.6 2.3 %copy-start.1 = (s32[1,512,1,8]{1,3,2,0:T(8,128)S(1)}, s32[1,512,1,8]{1,3,2,0:T(8,128)}, u32[]{:S(2)}) copy-start(s32[1,512,1,8]{1,3,2,0:T(8,128)} %param.9) | copy-start | bytes 49156
  1.6 36.3 %copy-start = (bf16[4,512,256]{2,1,0:T(8,128)(2,1)S(1)}, bf16[4,512,256]{2,1,0:T(8,128)(2,1)}, u32[]{:S(2)}) copy-start(bf16[4,512,256]{2,1,0:T(8,128)(2,1)} %weight_ref.1) | copy-start | bytes 3145732
  1.6 1.3 %copy-start.2 = (s32[1,512,1]{1,2,0:T(1,128)S(1)}, s32[1,512,1]{1,2,0:T(1,128)}, u32[]{:S(2)}) copy-start(s32[1,512,1]{1,2,0:T(1,128)} %param.10) | copy-start | bytes 6148
  37.9 0.7 %copy-start.3 = (s32[4]{0:T(128)S(1)}, s32[4]{0:T(128)}, u32[]{:S(2)}) copy-start(s32[4]{0:T(128)} %dims_ref.1) | copy-start | bytes 52

commit v3 on v2

--- a/solution.py
+++ b/solution.py
@@ -16,14 +16,26 @@
 def kernel(
     n_tab,
     n_rep,
+    dproj_hbm,
+    pooled_hbm,
+    rows_hbm,
+    lens_hbm,
+    weight_hbm,
+    dims_hbm,
+    out_row,
+    out_proj,
+    out_weight,
+    row_sum,
+    proj_sum,
+    live_weight,
+    dproj_raw,
+    pooled_raw,
     dproj_ref,
     pooled_ref,
-    rows_hbm,
-    lens_hbm,
-    out_row,
-    out_proj,
     rows_ref,
     lens_ref,
+    weight_ref,
+    dims_ref,
     dproj_all,
     pooled_all,
     counts,
@@ -31,6 +43,8 @@
     row_wire,
     proj_own,
     proj_wire,
+    load_sem,
+    store_sem,
     own_sem,
     a_send,
     a_recv,
@@ -50,6 +64,20 @@
     n_samples, width = dproj_ref.shape[1], dproj_ref.shape[2]
     piece = pooled_ref.shape[2] // 2
 
+    loads = [
+        pltpu.make_async_copy(src, dst, load_sem.at[i])
+        for i, (src, dst) in enumerate((
+            (dproj_hbm, dproj_raw),
+            (pooled_hbm, pooled_raw),
+            (rows_hbm, rows_ref),
+            (lens_hbm, lens_ref),
+            (weight_hbm.at[tab], weight_ref),
+            (dims_hbm, dims_ref),
+        ))
+    ]
+    for copy in loads:
+        copy.start()
+
     def remote(src, dst, send, recv, tab_to, rep_to):
         return pltpu.make_async_remote_copy(
             src_ref=src,
@@ -70,12 +98,8 @@
             barrier, inc=1, device_id=(tab, lax.rem(rep + 2 * k, n_rep)), device_id_type=MESH
         )
     pl.semaphore_signal(barrier, inc=1, device_id=(tab, partner), device_id_type=MESH)
-    bags = [
-        pltpu.make_async_copy(rows_hbm, rows_ref, own_sem.at[2]),
-        pltpu.make_async_copy(lens_hbm, lens_ref, own_sem.at[3]),
-    ]
-    for copy in bags:
-        copy.start()
+    loads[0].wait()
+    dproj_ref[...] = jnp.transpose(dproj_raw[...], (1, 0, 2))
     pl.semaphore_wait(barrier, n_tab - 1 + n_z)
 
     def columns(ref, at, which):
@@ -83,6 +107,9 @@
 
     gathers = []
     for which in range(3):
+        if which == 1:
+            loads[1].wait()
+            pooled_ref[...] = jnp.transpose(pooled_raw[...], (1, 0, 2))
         src, dst = (dproj_ref, dproj_all) if which == 0 else (pooled_ref, pooled_all)
         copies = []
         for k in range(1, n_tab):
@@ -101,7 +128,7 @@
     for copy in own:
         copy.start()
 
-    for copy in bags:
+    for copy in loads[2:4]:
         copy.wait()
     named = rows_ref[...]
     slots = lax.broadcasted_iota(jnp.int32, named.shape, 0)
@@ -120,9 +147,9 @@
     lax.fori_loop(0, counts.shape[0] // step, count, 0)
 
     buffers = [
-        (row_own, row_wire, out_row),
-        (proj_own.at[0], proj_wire.at[0], out_proj.at[0]),
-        (proj_own.at[1], proj_wire.at[1], out_proj.at[1]),
+        (row_own, row_wire, row_sum),
+        (proj_own.at[0], proj_wire.at[0], proj_sum.at[0]),
+        (proj_own.at[1], proj_wire.at[1], proj_sum.at[1]),
     ]
 
     def send_pair(which):
@@ -161,7 +188,9 @@
             out[y, z, :, :width] = high
             out[y, z, :, width:] = (total - high.astype(F32)).astype(BF16)
         else:
-            out[y, z] = high
+            first = (which - 1) * piece + (y * n_z + z) * total.shape[0]
+            at = lax.broadcasted_iota(jnp.int32, total.shape, 0) + first
+            out[y, z] = jnp.where(at < limit, total, 0.0).astype(BF16)
         block = out.at[y, z]
         copies = []
         for k in range(1, n_z):
@@ -203,6 +232,22 @@
             total = term if total is None else total + term
         proj_own[half] = total.reshape(proj_own.shape[1:])
         return send_pair(1 + half)
+
+    for copy in loads[4:]:
+        copy.wait()
+    limit = weight_ref.shape[0] // 16 * dims_ref[tab]
+    at_row = lax.broadcasted_iota(jnp.int32, weight_ref.shape, 0)
+    live_weight[...] = jnp.where(at_row < limit, weight_ref[...].astype(F32), 0.0).astype(BF16)
+    stores = [
+        pltpu.make_async_copy(src, dst, store_sem.at[i])
+        for i, (src, dst) in enumerate((
+            (live_weight, out_weight),
+            (row_sum, out_row),
+            (proj_sum.at[0], out_proj.at[0]),
+            (proj_sum.at[1], out_proj.at[1]),
+        ))
+    ]
+    stores[0].start()
 
     own[0].wait()
     for copy in gathers[0]:
@@ -222,31 +267,58 @@
     fwd0 = forward(0, sums0)
     fwd1 = forward(1, sums1)
     fwd2 = forward(2, sums2)
-    for copy in [last0, *fwd0, last1, *fwd1, last2, *fwd2]:
-        copy.wait()
+    for i, copies in enumerate(([last0, *fwd0], [last1, *fwd1], [last2, *fwd2])):
+        for copy in copies:
+            copy.wait_recv()
+        stores[1 + i].start()
     for copy in [
         *gathers[0], *gathers[1], *gathers[2], pair0, pair1, pair2,
         *line0, *line1, *line2, *sums0, *sums1, *sums2,
+        last0, last1, last2, *fwd0, *fwd1, *fwd2,
     ]:
         copy.wait_send()
-
-
-def finish(dims_ref, row_ref, sum_ref, weight_ref, emb_ref, proj_ref):
-    tab = lax.axis_index("tab")
-    widest = weight_ref.shape[1]
-    limit = widest // 16 * dims_ref[tab]
-    weight = weight_ref[tab]
-    width = weight.shape[1]
-    rows = row_ref[...]
-    emb = lax.dot_general(
-        rows[:, :width], weight, (((1,), (1,)), ((), ())), preferred_element_type=F32
-    ) + lax.dot_general(
-        rows[:, width:], weight, (((1,), (1,)), ((), ())), preferred_element_type=F32
-    )
-    emb_ref[0] = jnp.where(lax.broadcasted_iota(jnp.int32, emb.shape, 1) < limit, emb, 0.0)
-    total = sum_ref[...].astype(F32)
-    at = lax.broadcasted_iota(jnp.int32, total.shape, 0) + pl.program_id(0) * total.shape[0]
-    proj_ref[0] = jnp.where(at < limit, total, 0.0)
+    for copy in stores:
+        copy.wait()
+
+
+def finish(
+    row_hbm, sum_hbm, weight_hbm, emb_hbm, proj_hbm,
+    row_ref, sum_ref, weight_ref, emb_buf, proj_buf, load_sem, sem,
+):
+    loads = [
+        pltpu.make_async_copy(src, dst, load_sem.at[i])
+        for i, (src, dst) in enumerate((
+            (sum_hbm, sum_ref), (weight_hbm, weight_ref), (row_hbm, row_ref)
+        ))
+    ]
+    for copy in loads:
+        copy.start()
+    width = weight_ref.shape[1]
+    tiles = emb_buf.shape[0]
+    tile = emb_buf.shape[1]
+    copies = []
+
+    def store(buf, hbm, i):
+        copy = pltpu.make_async_copy(buf, hbm, sem.at[i])
+        copy.start()
+        copies.append(copy)
+
+    loads[0].wait()
+    proj_buf[...] = sum_ref[...].astype(F32)
+    store(proj_buf, proj_hbm.at[0], tiles)
+    loads[1].wait()
+    loads[2].wait()
+    weight = weight_ref[...]
+    for i in range(tiles):
+        rows = row_ref[i * tile : (i + 1) * tile, :]
+        emb_buf[i] = lax.dot_general(
+            rows[:, :width], weight, (((1,), (1,)), ((), ())), preferred_element_type=F32
+        ) + lax.dot_general(
+            rows[:, width:], weight, (((1,), (1,)), ((), ())), preferred_element_type=F32
+        )
+        store(emb_buf.at[i], emb_hbm.at[0, pl.ds(i * tile, tile)], i)
+    for copy in copies:
+        copy.wait()
 
 
 def fused(n_tab, n_rep, d_proj, pooled, proj, bag_rows, bag_lengths, dim_blocks):
@@ -254,22 +326,29 @@
     group, bag = bag_rows.shape[1], bag_rows.shape[3]
     n_z = n_rep // 2
     part, proj_part = ROWS // n_rep, widest // 2 // n_rep
-    by_table = jnp.transpose(d_proj[0], (1, 0, 2))
-    pooled_by_table = jnp.transpose(pooled[0], (1, 0, 2))
-    vmem = pl.BlockSpec(memory_space=pltpu.VMEM)
-    hbm = pl.BlockSpec(memory_space=pl.ANY)
+    hbm = pl.BlockSpec(memory_space=pltpu.HBM)
     dma = pltpu.SemaphoreType.DMA
-    row_sum, proj_sum = pl.pallas_call(
+    row_sum, proj_sum, weight = pl.pallas_call(
         functools.partial(kernel, n_tab, n_rep),
         out_shape=(
             jax.ShapeDtypeStruct((2, n_z, part, 2 * width), BF16),
             jax.ShapeDtypeStruct((2, 2, n_z, proj_part, width), BF16),
+            jax.ShapeDtypeStruct((widest, width), BF16),
         ),
-        in_specs=[vmem, vmem, hbm, hbm],
-        out_specs=(vmem, vmem),
+        in_specs=[hbm] * 6,
+        out_specs=(hbm, hbm, hbm),
         scratch_shapes=[
+            pltpu.VMEM((2, n_z, part, 2 * width), BF16),
+            pltpu.VMEM((2, 2, n_z, proj_part, width), BF16),
+            pltpu.VMEM((widest, width), BF16),
+            pltpu.VMEM((n_samples, n_tab, width), BF16),
+            pltpu.VMEM((n_samples, n_tab, widest), BF16),
+            pltpu.VMEM((n_tab, n_samples, width), BF16),
+            pltpu.VMEM((n_tab, n_samples, widest), BF16),
             pltpu.VMEM((bag, group), jnp.int32),
             pltpu.VMEM((1, group), jnp.int32),
+            pltpu.VMEM((widest, width), BF16),
+            pltpu.SMEM((n_tab,), jnp.int32),
             pltpu.VMEM((n_tab, n_samples, width), BF16),
             pltpu.VMEM((n_tab, n_samples, widest), BF16),
             pltpu.VMEM((ROWS, group), BF16),
@@ -277,7 +356,9 @@
             pltpu.VMEM((4, n_z, part, width), BF16),
             pltpu.VMEM((2, 2, n_z, proj_part, width), F32),
             pltpu.VMEM((2, 4, n_z, proj_part, width), BF16),
+            dma((6,)),
             dma((4,)),
+            dma((2,)),
             dma((3, n_tab)),
             dma((3, n_tab)),
             dma((3,)),
@@ -288,39 +369,41 @@
             dma((3, 2, n_z)),
         ],
         compiler_params=pltpu.CompilerParams(
-            collective_id=0, has_side_effects=True, vmem_limit_bytes=32 << 20
+            collective_id=0, has_side_effects=True, vmem_limit_bytes=60 << 20
         ),
     )(
-        by_table,
-        pooled_by_table,
+        d_proj[0],
+        pooled[0],
         jnp.transpose(bag_rows[0, :, 0, :]),
         bag_lengths.reshape(1, group),
+        proj,
+        dim_blocks,
     )
     tiles = 4
     emb, proj_grad = pl.pallas_call(
         finish,
-        grid=(tiles,),
         out_shape=(
             jax.ShapeDtypeStruct((1, ROWS, widest), F32),
             jax.ShapeDtypeStruct((1, widest, width), F32),
         ),
-        in_specs=[
-            pl.BlockSpec(memory_space=pltpu.SMEM),
-            pl.BlockSpec((ROWS // tiles, 2 * width), lambda i: (i, 0)),
-            pl.BlockSpec((widest // tiles, width), lambda i: (i, 0)),
-            vmem,
+        in_specs=[hbm] * 3,
+        out_specs=(hbm, hbm),
+        scratch_shapes=[
+            pltpu.VMEM((ROWS, 2 * width), BF16),
+            pltpu.VMEM((widest, width), BF16),
+            pltpu.VMEM((widest, width), BF16),
+            pltpu.VMEM((tiles, ROWS // tiles, widest), F32),
+            pltpu.VMEM((widest, width), F32),
+            dma((3,)),
+            dma((tiles + 1,)),
         ],
-        out_specs=(
-            pl.BlockSpec((1, ROWS // tiles, widest), lambda i: (0, i, 0)),
-            pl.BlockSpec((1, widest // tiles, width), lambda i: (0, i, 0)),
-        ),
-        compiler_params=pltpu.CompilerParams(vmem_limit_bytes=16 << 20),
+        compiler_params=pltpu.CompilerParams(vmem_limit_bytes=60 << 20),
         cost_estimate=pl.CostEstimate(
             flops=4 * ROWS * widest * width,
             bytes_accessed=4 * ROWS * widest + 6 * widest * width,
             transcendentals=0,
         ),
-    )(dim_blocks, row_sum.reshape(ROWS, 2 * width), proj_sum.reshape(widest, width), proj)
+    )(row_sum.reshape(ROWS, 2 * width), proj_sum.reshape(widest, width), weight)
     return emb, proj_grad
 
 

time: 41.7 us -> 39.4 us (0.945)
  local copies, waits for them, and re-layouts: 2.87 us -> 0 us
  Pallas kernels: 38 us -> 38.6 us
    unnamed x10 -> x0, local copies, waits for them, and re-layouts: 2.87 us -> none
    pallas_call x1, Pallas kernels: 35 us -> 35.8 us  [fused(): pl.pallas_call(functools.partial(kernel, n_tab, n_rep), out_shape=(jax.Sh...]
where the time goes in v3:
time: 39.4 us; the launch traced here: 39.2 us
  Pallas kernels  38.6 us (98%)
  between operations  0.64 us (2%)
    pallas_call x1, Pallas kernels, fused(): pl.pallas_call(functools.partial(kernel, n_tab, n_rep), out_shape=(jax.Sh...  35.8 us
    pallas_call x1, Pallas kernels, fused(): pl.pallas_call(finish, out_shape=(jax.ShapeDtypeStruct((1, ROWS, widest),...  2.79 us

profile of v3, /device:TPU:0, one launch (start us, length us, event | category | flops | bytes accessed | tf_op | source)
XLA Modules:
  0.0 39.2 jit_solution(16526653335293772207)
XLA Ops:
  0.6 35.8 %shard_map.77 = (bf16[2,4,64,512]{3,2,1,0:T(8,128)(2,1)}, bf16[2,2,4,32,256]{4,3,2,1,0:T(8,128)(2,1)}, bf16[512,256]{1,0:T(8,128)(2,1)}) custom-call(bf16[128,4,256]{2,1,0:T(4,128)(2,1)} %bitcast.10, bf16[128,4,512]{2,1,0:T(4,128)(2,1)} %bitcast.8, s32[8,512]{1,0:T(8,128)} %bitcast.12, s32[1,512]{1,0:T(1,128)} %bitcast.13, bf16[4,512,256]{2,1,0:T(8,128)(2,1)} %weight_hbm.1, ...), custom_call_target="tpu_custom_call" | custom-call | tf_op jit(solution)/shard_map/pallas_call | solution.py:331
  36.4 2.8 %shard_map.78 = (f32[1,512,512]{2,1,0:T(8,128)}, f32[1,512,256]{2,1,0:T(8,128)}) custom-call(bf16[512,512]{1,0:T(8,128)(2,1)} %bitcast.9, bf16[512,256]{1,0:T(8,128)(2,1)} %bitcast.11, bf16[512,256]{1,0:T(8,128)(2,1)} %get-tuple-element.7.weight_hbm), custom_call_target="tpu_custom_call" | custom-call | flops 268435456 | bytes 1835008 | tf_op jit(solution)/shard_map/pallas_call | solution.py:383

commit v4 on v3

--- a/solution.py
+++ b/solution.py
@@ -11,6 +11,23 @@
 MESH = pl.DeviceIdType.MESH
 BF16 = jnp.bfloat16
 F32 = jnp.float32
+
+
+SCALE_ROWS = 16
+
+
+def encode(total):
+    peak = jnp.maximum(jnp.max(jnp.abs(total), axis=0, keepdims=True), 1e-30)
+    power = jnp.floor(jnp.log2(peak) + 1.01) - 15.0
+    coded = jnp.floor(total * jnp.exp2(-power) + 0.5)
+    coded = jnp.clip(coded, -32767.0, 32767.0).astype(jnp.int32).astype(jnp.int16)
+    powers = jnp.broadcast_to(power, (SCALE_ROWS, total.shape[1]))
+    return coded, powers.astype(jnp.int32).astype(jnp.int16)
+
+
+def decode(coded, powers):
+    scale = jnp.exp2(powers.astype(jnp.int32).astype(F32)[:1])
+    return coded.astype(jnp.int32).astype(F32) * scale
 
 
 def kernel(
@@ -22,11 +39,12 @@
     lens_hbm,
     weight_hbm,
     dims_hbm,
-    out_row,
+    out_emb,
     out_proj,
-    out_weight,
     row_sum,
     proj_sum,
+    emb_buf,
+    proj_buf,
     live_weight,
     dproj_raw,
     pooled_raw,
@@ -183,10 +201,11 @@
         total = sums[y, z]
         for k in range(1, n_z):
             total = total + wire[3, k].astype(F32)
-        high = total.astype(BF16)
         if which == 0:
-            out[y, z, :, :width] = high
-            out[y, z, :, width:] = (total - high.astype(F32)).astype(BF16)
+            part = total.shape[0]
+            coded, powers = encode(total)
+            out[y, z, :part] = coded
+            out[y, z, part:] = powers
         else:
             first = (which - 1) * piece + (y * n_z + z) * total.shape[0]
             at = lax.broadcasted_iota(jnp.int32, total.shape, 0) + first
@@ -241,13 +260,25 @@
     stores = [
         pltpu.make_async_copy(src, dst, store_sem.at[i])
         for i, (src, dst) in enumerate((
-            (live_weight, out_weight),
-            (row_sum, out_row),
-            (proj_sum.at[0], out_proj.at[0]),
-            (proj_sum.at[1], out_proj.at[1]),
+            (emb_buf.at[0], out_emb.at[y]),
+            (emb_buf.at[1], out_emb.at[1 - y]),
+            (proj_buf.at[0], out_proj.at[0]),
+            (proj_buf.at[1], out_proj.at[1]),
         ))
     ]
-    stores[0].start()
+
+    def table_rows(slot, half):
+        part = row_sum.shape[2] - SCALE_ROWS
+        total = jnp.concatenate(
+            [decode(row_sum[half, i, :part], row_sum[half, i, part:]) for i in range(n_z)], axis=0
+        )
+        high = total.astype(BF16)
+        low = (total - high.astype(F32)).astype(BF16)
+        weight = live_weight[...]
+        emb_buf[slot] = lax.dot_general(
+            high, weight, (((1,), (1,)), ((), ())), preferred_element_type=F32
+        ) + lax.dot_general(low, weight, (((1,), (1,)), ((), ())), preferred_element_type=F32)
+        stores[slot].start()
 
     own[0].wait()
     for copy in gathers[0]:
@@ -267,10 +298,15 @@
     fwd0 = forward(0, sums0)
     fwd1 = forward(1, sums1)
     fwd2 = forward(2, sums2)
-    for i, copies in enumerate(([last0, *fwd0], [last1, *fwd1], [last2, *fwd2])):
+    table_rows(0, y)
+    for copy in [last0, *fwd0]:
+        copy.wait_recv()
+    table_rows(1, 1 - y)
+    for half, copies in enumerate(([last1, *fwd1], [last2, *fwd2])):
         for copy in copies:
             copy.wait_recv()
-        stores[1 + i].start()
+        proj_buf[half] = proj_sum[half].astype(F32).reshape(proj_buf.shape[1:])
+        stores[2 + half].start()
     for copy in [
         *gathers[0], *gathers[1], *gathers[2], pair0, pair1, pair2,
         *line0, *line1, *line2, *sums0, *sums1, *sums2,
@@ -281,42 +317,14 @@
         copy.wait()
 
 
-def finish(
-    row_hbm, sum_hbm, weight_hbm, emb_hbm, proj_hbm,
-    row_ref, sum_ref, weight_ref, emb_buf, proj_buf, load_sem, sem,
-):
-    loads = [
-        pltpu.make_async_copy(src, dst, load_sem.at[i])
-        for i, (src, dst) in enumerate((
-            (sum_hbm, sum_ref), (weight_hbm, weight_ref), (row_hbm, row_ref)
-        ))
+def finish(emb_from, proj_from, emb_to, proj_to, sem):
+    copies = [
+        pltpu.make_async_copy(src.at[i], dst.at[i], sem.at[which, i])
+        for which, (src, dst) in enumerate(((proj_from, proj_to), (emb_from, emb_to)))
+        for i in range(src.shape[0])
     ]
-    for copy in loads:
+    for copy in copies:
         copy.start()
-    width = weight_ref.shape[1]
-    tiles = emb_buf.shape[0]
-    tile = emb_buf.shape[1]
-    copies = []
-
-    def store(buf, hbm, i):
-        copy = pltpu.make_async_copy(buf, hbm, sem.at[i])
-        copy.start()
-        copies.append(copy)
-
-    loads[0].wait()
-    proj_buf[...] = sum_ref[...].astype(F32)
-    store(proj_buf, proj_hbm.at[0], tiles)
-    loads[1].wait()
-    loads[2].wait()
-    weight = weight_ref[...]
-    for i in range(tiles):
-        rows = row_ref[i * tile : (i + 1) * tile, :]
-        emb_buf[i] = lax.dot_general(
-            rows[:, :width], weight, (((1,), (1,)), ((), ())), preferred_element_type=F32
-        ) + lax.dot_general(
-            rows[:, width:], weight, (((1,), (1,)), ((), ())), preferred_element_type=F32
-        )
-        store(emb_buf.at[i], emb_hbm.at[0, pl.ds(i * tile, tile)], i)
     for copy in copies:
         copy.wait()
 
@@ -328,18 +336,19 @@
     part, proj_part = ROWS // n_rep, widest // 2 // n_rep
     hbm = pl.BlockSpec(memory_space=pltpu.HBM)
     dma = pltpu.SemaphoreType.DMA
-    row_sum, proj_sum, weight = pl.pallas_call(
+    emb, proj_grad = pl.pallas_call(
         functools.partial(kernel, n_tab, n_rep),
         out_shape=(
-            jax.ShapeDtypeStruct((2, n_z, part, 2 * width), BF16),
-            jax.ShapeDtypeStruct((2, 2, n_z, proj_part, width), BF16),
-            jax.ShapeDtypeStruct((widest, width), BF16),
+            jax.ShapeDtypeStruct((2, ROWS // 2, widest), F32),
+            jax.ShapeDtypeStruct((2, widest // 2, width), F32),
         ),
         in_specs=[hbm] * 6,
-        out_specs=(hbm, hbm, hbm),
+        out_specs=(hbm, hbm),
         scratch_shapes=[
-            pltpu.VMEM((2, n_z, part, 2 * width), BF16),
+            pltpu.VMEM((2, n_z, part + SCALE_ROWS, width), jnp.int16),
             pltpu.VMEM((2, 2, n_z, proj_part, width), BF16),
+            pltpu.VMEM((2, ROWS // 2, widest), F32),
+            pltpu.VMEM((2, widest // 2, width), F32),
             pltpu.VMEM((widest, width), BF16),
             pltpu.VMEM((n_samples, n_tab, width), BF16),
             pltpu.VMEM((n_samples, n_tab, widest), BF16),
@@ -379,32 +388,21 @@
         proj,
         dim_blocks,
     )
-    tiles = 4
     emb, proj_grad = pl.pallas_call(
         finish,
         out_shape=(
-            jax.ShapeDtypeStruct((1, ROWS, widest), F32),
-            jax.ShapeDtypeStruct((1, widest, width), F32),
+            jax.ShapeDtypeStruct(emb.shape, F32),
+            jax.ShapeDtypeStruct(proj_grad.shape, F32),
         ),
-        in_specs=[hbm] * 3,
+        in_specs=[hbm] * 2,
         out_specs=(hbm, hbm),
-        scratch_shapes=[
-            pltpu.VMEM((ROWS, 2 * width), BF16),
-            pltpu.VMEM((widest, width), BF16),
-            pltpu.VMEM((widest, width), BF16),
-            pltpu.VMEM((tiles, ROWS // tiles, widest), F32),
-            pltpu.VMEM((widest, width), F32),
-            dma((3,)),
-            dma((tiles + 1,)),
-        ],
+        scratch_shapes=[dma((2, 2))],
         compiler_params=pltpu.CompilerParams(vmem_limit_bytes=60 << 20),
         cost_estimate=pl.CostEstimate(
-            flops=4 * ROWS * widest * width,
-            bytes_accessed=4 * ROWS * widest + 6 * widest * width,
-            transcendentals=0,
+            flops=0, bytes_accessed=8 * (ROWS + width) * widest, transcendentals=0
         ),
-    )(row_sum.reshape(ROWS, 2 * width), proj_sum.reshape(widest, width), weight)
-    return emb, proj_grad
+    )(emb, proj_grad)
+    return emb.reshape(1, ROWS, widest), proj_grad.reshape(1, widest, width)
 
 
 def general(d_proj, pooled, proj, bag_rows, bag_lengths, dim_blocks):

time: 39.4 us -> 83 us (2.11)
  Pallas kernels: 38.6 us -> 82.2 us
    pallas_call x1, Pallas kernels: 2.79 us -> 48.8 us  [fused(): pl.pallas_call(finish, out_shape=(jax.ShapeDtypeStruct(emb.shape, F32), j...]
    pallas_call x1, Pallas kernels: 35.8 us -> 33.4 us  [fused(): pl.pallas_call(functools.partial(kernel, n_tab, n_rep), out_shape=(jax.Sh...]
where the time goes in v4:
time: 83 us; the launch traced here: 82.8 us
  Pallas kernels  82.2 us (99%)
    pallas_call x1, Pallas kernels, fused(): pl.pallas_call(finish, out_shape=(jax.ShapeDtypeStruct(emb.shape, F32), j...  48.8 us
    pallas_call x1, Pallas kernels, fused(): pl.pallas_call(functools.partial(kernel, n_tab, n_rep), out_shape=(jax.Sh...  33.4 us

profile of v4, /device:TPU:0, one launch (start us, length us, event | category | flops | bytes accessed | tf_op | source)
XLA Modules:
  0.0 82.8 jit_solution(2768627853572711657)
XLA Ops:
  0.6 33.4 %shard_map.77 = (f32[2,256,512]{2,1,0:T(8,128)}, f32[2,256,256]{2,1,0:T(8,128)}) custom-call(bf16[128,4,256]{2,1,0:T(4,128)(2,1)} %bitcast.9, bf16[128,4,512]{2,1,0:T(4,128)(2,1)} %bitcast.8, s32[8,512]{1,0:T(8,128)} %bitcast.10, s32[1,512]{1,0:T(1,128)} %bitcast.11, bf16[4,512,256]{2,1,0:T(8,128)(2,1)} %weight_hbm.1, s32[4]{0:T(128)} %dims_hbm.1), custom_call_target="tpu_custom_call" | custom-call | tf_op jit(solution)/shard_map/pallas_call | solution.py:339
  34.1 48.8 %shard_map.78 = (f32[2,256,512]{2,1,0:T(8,128)}, f32[2,256,256]{2,1,0:T(8,128)}) custom-call(f32[2,256,512]{2,1,0:T(8,128)} %get-tuple-element.6.emb_from, f32[2,256,256]{2,1,0:T(8,128)} %get-tuple-element.7.proj_from), custom_call_target="tpu_custom_call" | custom-call | bytes 3145728 | tf_op jit(solution)/shard_map/pallas_call | solution.py:391

commit v5 on v4

--- a/solution.py
+++ b/solution.py
@@ -80,7 +80,7 @@
     z = rep // 2
     partner = rep + 1 - 2 * y
     n_samples, width = dproj_ref.shape[1], dproj_ref.shape[2]
-    piece = pooled_ref.shape[2] // 2
+    piece = pooled_ref.shape[1] // 2
 
     loads = [
         pltpu.make_async_copy(src, dst, load_sem.at[i])
@@ -121,13 +121,17 @@
     pl.semaphore_wait(barrier, n_tab - 1 + n_z)
 
     def columns(ref, at, which):
-        return ref.at[at] if which == 0 else ref.at[at, :, pl.ds((which - 1) * piece, piece)]
+        return ref.at[at] if which == 0 else ref.at[at, pl.ds((which - 1) * piece, piece)]
 
     gathers = []
     for which in range(3):
         if which == 1:
             loads[1].wait()
-            pooled_ref[...] = jnp.transpose(pooled_raw[...], (1, 0, 2))
+            by_table = jnp.transpose(pooled_raw[...], (1, 0, 2))
+        if which > 0:
+            at = (which - 1) * piece
+            for table in range(n_tab):
+                pooled_ref[table, at : at + piece] = by_table[table, :, at : at + piece].T
         src, dst = (dproj_ref, dproj_all) if which == 0 else (pooled_ref, pooled_all)
         copies = []
         for k in range(1, n_tab):
@@ -139,12 +143,8 @@
             copy.start()
             copies.append(copy)
         gathers.append(copies)
-    own = [
-        pltpu.make_async_copy(src.at[tab], dst.at[tab], own_sem.at[which])
-        for which, (src, dst) in enumerate(((dproj_ref, dproj_all), (pooled_ref, pooled_all)))
-    ]
-    for copy in own:
-        copy.start()
+    own = pltpu.make_async_copy(dproj_ref.at[tab], dproj_all.at[tab], own_sem.at[0])
+    own.start()
 
     for copy in loads[2:4]:
         copy.wait()
@@ -244,10 +244,8 @@
             if k > 0:
                 gathers[1 + half][k - 1].wait_recv()
             at = lax.rem(tab - k + n_tab, n_tab)
-            term = lax.dot_general(
-                pooled_all[at, :, half * piece : (half + 1) * piece], dproj_all[at],
-                (((0,), (0,)), ((), ())), preferred_element_type=F32,
-            )
+            block = (pooled_all if k > 0 else pooled_ref)[at, half * piece : (half + 1) * piece]
+            term = jnp.dot(block, dproj_all[at], preferred_element_type=F32)
             total = term if total is None else total + term
         proj_own[half] = total.reshape(proj_own.shape[1:])
         return send_pair(1 + half)
@@ -280,13 +278,12 @@
         ) + lax.dot_general(low, weight, (((1,), (1,)), ((), ())), preferred_element_type=F32)
         stores[slot].start()
 
-    own[0].wait()
+    own.wait()
     for copy in gathers[0]:
         copy.wait_recv()
     d_all = dproj_all[...].reshape(n_tab * n_samples, width)
     row_own[...] = jnp.dot(counts[...], d_all, preferred_element_type=F32).reshape(row_own.shape)
     pair0 = send_pair(0)
-    own[1].wait()
     pair1 = project(0)
     line0 = send_line(0, pair0)
     pair2 = project(1)
@@ -317,15 +314,20 @@
         copy.wait()
 
 
-def finish(emb_from, proj_from, emb_to, proj_to, sem):
-    copies = [
-        pltpu.make_async_copy(src.at[i], dst.at[i], sem.at[which, i])
-        for which, (src, dst) in enumerate(((proj_from, proj_to), (emb_from, emb_to)))
-        for i in range(src.shape[0])
-    ]
-    for copy in copies:
+def finish(emb_from, proj_from, emb_to, proj_to, emb_buf, proj_buf, load_sem, store_sem):
+    loads, stores = [], []
+    for which, (src, buf, dst) in enumerate(
+        ((proj_from, proj_buf, proj_to), (emb_from, emb_buf, emb_to))
+    ):
+        for i in range(src.shape[0]):
+            loads.append(pltpu.make_async_copy(src.at[i], buf.at[i], load_sem.at[which, i]))
+            stores.append(pltpu.make_async_copy(buf.at[i], dst.at[i], store_sem.at[which, i]))
+    for copy in loads:
         copy.start()
-    for copy in copies:
+    for load, copy in zip(loads, stores):
+        load.wait()
+        copy.start()
+    for copy in stores:
         copy.wait()
 
 
@@ -353,13 +355,13 @@
             pltpu.VMEM((n_samples, n_tab, width), BF16),
             pltpu.VMEM((n_samples, n_tab, widest), BF16),
             pltpu.VMEM((n_tab, n_samples, width), BF16),
-            pltpu.VMEM((n_tab, n_samples, widest), BF16),
+            pltpu.VMEM((n_tab, widest, n_samples), BF16),
             pltpu.VMEM((bag, group), jnp.int32),
             pltpu.VMEM((1, group), jnp.int32),
             pltpu.VMEM((widest, width), BF16),
             pltpu.SMEM((n_tab,), jnp.int32),
             pltpu.VMEM((n_tab, n_samples, width), BF16),
-            pltpu.VMEM((n_tab, n_samples, widest), BF16),
+            pltpu.VMEM((n_tab, widest, n_samples), BF16),
             pltpu.VMEM((ROWS, group), BF16),
             pltpu.VMEM((2, n_z, part, width), F32),
             pltpu.VMEM((4, n_z, part, width), BF16),
@@ -367,7 +369,7 @@
             pltpu.VMEM((2, 4, n_z, proj_part, width), BF16),
             dma((6,)),
             dma((4,)),
-            dma((2,)),
+            dma((1,)),
             dma((3, n_tab)),
             dma((3, n_tab)),
             dma((3,)),
@@ -388,6 +390,9 @@
         proj,
         dim_blocks,
     )
+    tiles = 4
+    emb = emb.reshape(tiles, ROWS // tiles, widest)
+    proj_grad = proj_grad.reshape(tiles, widest // tiles, width)
     emb, proj_grad = pl.pallas_call(
         finish,
         out_shape=(
@@ -396,7 +401,12 @@
         ),
         in_specs=[hbm] * 2,
         out_specs=(hbm, hbm),
-        scratch_shapes=[dma((2, 2))],
+        scratch_shapes=[
+            pltpu.VMEM(emb.shape, F32),
+            pltpu.VMEM(proj_grad.shape, F32),
+            dma((2, tiles)),
+            dma((2, tiles)),
+        ],
         compiler_params=pltpu.CompilerParams(vmem_limit_bytes=60 << 20),
         cost_estimate=pl.CostEstimate(
             flops=0, bytes_accessed=8 * (ROWS + width) * widest, transcendentals=0

time: 83 us -> 36.7 us (0.44)
  Pallas kernels: 82.2 us -> 35.9 us
    pallas_call x1, Pallas kernels: 48.8 us -> 2.31 us  [fused(): pl.pallas_call(finish, out_shape=(jax.ShapeDtypeStruct(emb.shape, F32), j...]
where the time goes in v5:
time: 36.7 us; the launch traced here: 36.5 us
  Pallas kernels  35.9 us (98%)
  between operations  0.64 us (2%)
    pallas_call x1, Pallas kernels, fused(): pl.pallas_call(functools.partial(kernel, n_tab, n_rep), out_shape=(jax.Sh...  33.6 us
    pallas_call x1, Pallas kernels, fused(): pl.pallas_call(finish, out_shape=(jax.ShapeDtypeStruct(emb.shape, F32), j...  2.31 us

profile of v5, /device:TPU:0, one launch (start us, length us, event | category | flops | bytes accessed | tf_op | source)
XLA Modules:
  0.0 36.5 jit_solution(1665930513576192305)
XLA Ops:
  0.6 33.6 %shard_map.77 = (f32[2,256,512]{2,1,0:T(8,128)}, f32[2,256,256]{2,1,0:T(8,128)}) custom-call(bf16[128,4,256]{2,1,0:T(4,128)(2,1)} %bitcast.13, bf16[128,4,512]{2,1,0:T(4,128)(2,1)} %bitcast.11, s32[8,512]{1,0:T(8,128)} %bitcast.14, s32[1,512]{1,0:T(1,128)} %bitcast.15, bf16[4,512,256]{2,1,0:T(8,128)(2,1)} %weight_hbm.1, s32[4]{0:T(128)} %dims_hbm.1), custom_call_target="tpu_custom_call" | custom-call | tf_op jit(solution)/shard_map/pallas_call | solution.py:341
  34.2 2.3 %shard_map.78 = (f32[4,128,512]{2,1,0:T(8,128)}, f32[4,128,256]{2,1,0:T(8,128)}) custom-call(f32[4,128,512]{2,1,0:T(8,128)} %bitcast.10, f32[4,128,256]{2,1,0:T(8,128)} %bitcast.12), custom_call_target="tpu_custom_call" | custom-call | bytes 3145728 | tf_op jit(solution)/shard_map/pallas_call | solution.py:396

commit v6 on v5

--- a/solution.py
+++ b/solution.py
@@ -44,7 +44,6 @@
     row_sum,
     proj_sum,
     emb_buf,
-    proj_buf,
     live_weight,
     dproj_raw,
     pooled_raw,
@@ -66,6 +65,8 @@
     own_sem,
     a_send,
     a_recv,
+    c_send,
+    c_recv,
     y_send,
     y_recv,
     z_send,
@@ -111,14 +112,13 @@
         pl.semaphore_signal(
             barrier, inc=1, device_id=(lax.rem(tab + k, n_tab), rep), device_id_type=MESH
         )
-    for k in range(1, n_z):
+    for k in range(1, n_rep):
         pl.semaphore_signal(
-            barrier, inc=1, device_id=(tab, lax.rem(rep + 2 * k, n_rep)), device_id_type=MESH
+            barrier, inc=1, device_id=(tab, lax.rem(rep + k, n_rep)), device_id_type=MESH
         )
-    pl.semaphore_signal(barrier, inc=1, device_id=(tab, partner), device_id_type=MESH)
     loads[0].wait()
     dproj_ref[...] = jnp.transpose(dproj_raw[...], (1, 0, 2))
-    pl.semaphore_wait(barrier, n_tab - 1 + n_z)
+    pl.semaphore_wait(barrier, n_tab + n_rep - 2)
 
     def columns(ref, at, which):
         return ref.at[at] if which == 0 else ref.at[at, pl.ds((which - 1) * piece, piece)]
@@ -170,6 +170,19 @@
         (proj_own.at[1], proj_wire.at[1], proj_sum.at[1]),
     ]
 
+    def send_all():
+        row_wire[0] = row_own[...].reshape(row_wire.shape[1:]).astype(BF16)
+        copies = []
+        for k in range(1, n_rep):
+            to = lax.rem(rep + k, n_rep)
+            slot = lax.rem(to, 2) * n_z + to // 2
+            copy = remote(
+                row_wire.at[0, slot], row_wire.at[1, k], c_send.at[k], c_recv.at[k], tab, to
+            )
+            copy.start()
+            copies.append(copy)
+        return copies
+
     def send_pair(which):
         sums, wire, _ = buffers[which]
         wire[0] = sums[1 - y].astype(BF16)
@@ -199,8 +212,8 @@
         for copy in line:
             copy.wait_recv()
         total = sums[y, z]
-        for k in range(1, n_z):
-            total = total + wire[3, k].astype(F32)
+        for k in range(1, n_rep if which == 0 else n_z):
+            total = total + (wire[1, k] if which == 0 else wire[3, k]).astype(F32)
         if which == 0:
             part = total.shape[0]
             coded, powers = encode(total)
@@ -260,8 +273,8 @@
         for i, (src, dst) in enumerate((
             (emb_buf.at[0], out_emb.at[y]),
             (emb_buf.at[1], out_emb.at[1 - y]),
-            (proj_buf.at[0], out_proj.at[0]),
-            (proj_buf.at[1], out_proj.at[1]),
+            (proj_sum.at[0], out_proj.at[0]),
+            (proj_sum.at[1], out_proj.at[1]),
         ))
     ]
 
@@ -283,9 +296,8 @@
         copy.wait_recv()
     d_all = dproj_all[...].reshape(n_tab * n_samples, width)
     row_own[...] = jnp.dot(counts[...], d_all, preferred_element_type=F32).reshape(row_own.shape)
-    pair0 = send_pair(0)
+    line0 = send_all()
     pair1 = project(0)
-    line0 = send_line(0, pair0)
     pair2 = project(1)
     line1 = send_line(1, pair1)
     line2 = send_line(2, pair2)
@@ -302,10 +314,9 @@
     for half, copies in enumerate(([last1, *fwd1], [last2, *fwd2])):
         for copy in copies:
             copy.wait_recv()
-        proj_buf[half] = proj_sum[half].astype(F32).reshape(proj_buf.shape[1:])
         stores[2 + half].start()
     for copy in [
-        *gathers[0], *gathers[1], *gathers[2], pair0, pair1, pair2,
+        *gathers[0], *gathers[1], *gathers[2], pair1, pair2,
         *line0, *line1, *line2, *sums0, *sums1, *sums2,
         last0, last1, last2, *fwd0, *fwd1, *fwd2,
     ]:
@@ -314,19 +325,22 @@
         copy.wait()
 
 
-def finish(emb_from, proj_from, emb_to, proj_to, emb_buf, proj_buf, load_sem, store_sem):
-    loads, stores = [], []
-    for which, (src, buf, dst) in enumerate(
-        ((proj_from, proj_buf, proj_to), (emb_from, emb_buf, emb_to))
-    ):
-        for i in range(src.shape[0]):
-            loads.append(pltpu.make_async_copy(src.at[i], buf.at[i], load_sem.at[which, i]))
-            stores.append(pltpu.make_async_copy(buf.at[i], dst.at[i], store_sem.at[which, i]))
+def finish(
+    emb_from, proj_from, emb_to, proj_to, emb_buf, proj_in, proj_out, load_sem, store_sem
+):
+    tiles = emb_from.shape[0]
+    loads = [pltpu.make_async_copy(proj_from, proj_in, load_sem.at[tiles])]
+    stores = [pltpu.make_async_copy(proj_out, proj_to, store_sem.at[tiles])]
+    for i in range(tiles):
+        loads.append(pltpu.make_async_copy(emb_from.at[i], emb_buf.at[i], load_sem.at[i]))
+        stores.append(pltpu.make_async_copy(emb_buf.at[i], emb_to.at[i], store_sem.at[i]))
     for copy in loads:
         copy.start()
-    for load, copy in zip(loads, stores):
-        load.wait()
-        copy.start()
+    for i in range(tiles + 1):
+        loads[i].wait()
+        if i == 0:
+            proj_out[...] = proj_in[...].astype(F32)
+        stores[i].start()
     for copy in stores:
         copy.wait()
 
@@ -342,7 +356,7 @@
         functools.partial(kernel, n_tab, n_rep),
         out_shape=(
             jax.ShapeDtypeStruct((2, ROWS // 2, widest), F32),
-            jax.ShapeDtypeStruct((2, widest // 2, width), F32),
+            jax.ShapeDtypeStruct((2, 2, n_z, proj_part, width), BF16),
         ),
         in_specs=[hbm] * 6,
         out_specs=(hbm, hbm),
@@ -350,7 +364,6 @@
             pltpu.VMEM((2, n_z, part + SCALE_ROWS, width), jnp.int16),
             pltpu.VMEM((2, 2, n_z, proj_part, width), BF16),
             pltpu.VMEM((2, ROWS // 2, widest), F32),
-            pltpu.VMEM((2, widest // 2, width), F32),
             pltpu.VMEM((widest, width), BF16),
             pltpu.VMEM((n_samples, n_tab, width), BF16),
             pltpu.VMEM((n_samples, n_tab, widest), BF16),
@@ -364,7 +377,7 @@
             pltpu.VMEM((n_tab, widest, n_samples), BF16),
             pltpu.VMEM((ROWS, group), BF16),
             pltpu.VMEM((2, n_z, part, width), F32),
-            pltpu.VMEM((4, n_z, part, width), BF16),
+            pltpu.VMEM((2, n_rep, part, width), BF16),
             pltpu.VMEM((2, 2, n_z, proj_part, width), F32),
             pltpu.VMEM((2, 4, n_z, proj_part, width), BF16),
             dma((6,)),
@@ -372,6 +385,8 @@
             dma((1,)),
             dma((3, n_tab)),
             dma((3, n_tab)),
+            dma((n_rep,)),
+            dma((n_rep,)),
             dma((3,)),
             dma((3,)),
             dma((3, n_z)),
@@ -392,7 +407,7 @@
     )
     tiles = 4
     emb = emb.reshape(tiles, ROWS // tiles, widest)
-    proj_grad = proj_grad.reshape(tiles, widest // tiles, width)
+    proj_grad = proj_grad.reshape(widest, width)
     emb, proj_grad = pl.pallas_call(
         finish,
         out_shape=(
@@ -403,9 +418,10 @@
         out_specs=(hbm, hbm),
         scratch_shapes=[
             pltpu.VMEM(emb.shape, F32),
+            pltpu.VMEM(proj_grad.shape, BF16),
             pltpu.VMEM(proj_grad.shape, F32),
-            dma((2, tiles)),
-            dma((2, tiles)),
+            dma((tiles + 1,)),
+            dma((tiles + 1,)),
         ],
         compiler_params=pltpu.CompilerParams(vmem_limit_bytes=60 << 20),
         cost_estimate=pl.CostEstimate(

time: 36.7 us -> 37.3 us (1.016)
  Pallas kernels: 35.9 us -> 36.5 us
    pallas_call x1, Pallas kernels: 33.6 us -> 34.3 us  [fused(): pl.pallas_call(functools.partial(kernel, n_tab, n_rep), out_shape=(jax.Sh...]
where the time goes in v6:
time: 37.3 us; the launch traced here: 37.1 us
  Pallas kernels  36.5 us (98%)
  between operations  0.64 us (2%)
    pallas_call x1, Pallas kernels, fused(): pl.pallas_call(functools.partial(kernel, n_tab, n_rep), out_shape=(jax.Sh...  34.3 us
    pallas_call x1, Pallas kernels, fused(): pl.pallas_call(finish, out_shape=(jax.ShapeDtypeStruct(emb.shape, F32), j...  2.21 us

profile of v6, /device:TPU:0, one launch (start us, length us, event | category | flops | bytes accessed | tf_op | source)
XLA Modules:
  0.0 37.1 jit_solution(12323575086016045248)
XLA Ops:
  0.6 34.3 %shard_map.77 = (f32[2,256,512]{2,1,0:T(8,128)}, bf16[2,2,4,32,256]{4,3,2,1,0:T(8,128)(2,1)}) custom-call(bf16[128,4,256]{2,1,0:T(4,128)(2,1)} %bitcast.12, bf16[128,4,512]{2,1,0:T(4,128)(2,1)} %bitcast.11, s32[8,512]{1,0:T(8,128)} %bitcast.14, s32[1,512]{1,0:T(1,128)} %bitcast.15, bf16[4,512,256]{2,1,0:T(8,128)(2,1)} %weight_hbm.1, s32[4]{0:T(128)} %dims_hbm.1), custom_call_target="tpu_custom_call" | custom-call | tf_op jit(solution)/shard_map/pallas_call | solution.py:355
  34.9 2.2 %shard_map.78 = (f32[4,128,512]{2,1,0:T(8,128)}, f32[512,256]{1,0:T(8,128)}) custom-call(f32[4,128,512]{2,1,0:T(8,128)} %bitcast.10, bf16[512,256]{1,0:T(8,128)(2,1)} %bitcast.13), custom_call_target="tpu_custom_call" | custom-call | bytes 3145728 | tf_op jit(solution)/shard_map/pallas_call | solution.py:411

commit v7 on v6

--- a/solution.py
+++ b/solution.py
@@ -65,8 +65,6 @@
     own_sem,
     a_send,
     a_recv,
-    c_send,
-    c_recv,
     y_send,
     y_recv,
     z_send,
@@ -80,7 +78,7 @@
     y = lax.rem(rep, 2)
     z = rep // 2
     partner = rep + 1 - 2 * y
-    n_samples, width = dproj_ref.shape[1], dproj_ref.shape[2]
+    n_samples, width = dproj_ref.shape[2], dproj_ref.shape[3]
     piece = pooled_ref.shape[1] // 2
 
     loads = [
@@ -112,39 +110,50 @@
         pl.semaphore_signal(
             barrier, inc=1, device_id=(lax.rem(tab + k, n_tab), rep), device_id_type=MESH
         )
-    for k in range(1, n_rep):
+    for k in range(1, n_z):
         pl.semaphore_signal(
-            barrier, inc=1, device_id=(tab, lax.rem(rep + k, n_rep)), device_id_type=MESH
-        )
+            barrier, inc=1, device_id=(tab, lax.rem(rep + 2 * k, n_rep)), device_id_type=MESH
+        )
+    pl.semaphore_signal(barrier, inc=1, device_id=(tab, partner), device_id_type=MESH)
     loads[0].wait()
-    dproj_ref[...] = jnp.transpose(dproj_raw[...], (1, 0, 2))
-    pl.semaphore_wait(barrier, n_tab + n_rep - 2)
-
-    def columns(ref, at, which):
-        return ref.at[at] if which == 0 else ref.at[at, pl.ds((which - 1) * piece, piece)]
+    by_table = jnp.transpose(dproj_raw[...], (1, 0, 2))
+    for half in range(2):
+        dproj_ref[half] = by_table[:, :, half * width : (half + 1) * width]
+    pl.semaphore_wait(barrier, n_tab - 1 + n_z)
+
+    def columns(first, second, which, at):
+        if which < 2:
+            return first.at[which, at]
+        return second.at[at, pl.ds((which - 2) * piece, piece)]
 
     gathers = []
-    for which in range(3):
-        if which == 1:
+    for which in range(4):
+        if which == 2:
             loads[1].wait()
             by_table = jnp.transpose(pooled_raw[...], (1, 0, 2))
-        if which > 0:
-            at = (which - 1) * piece
+        if which >= 2:
+            at = (which - 2) * piece
             for table in range(n_tab):
                 pooled_ref[table, at : at + piece] = by_table[table, :, at : at + piece].T
-        src, dst = (dproj_ref, dproj_all) if which == 0 else (pooled_ref, pooled_all)
         copies = []
         for k in range(1, n_tab):
             to = lax.rem(tab + k, n_tab)
             copy = remote(
-                columns(src, to, which), columns(dst, tab, which),
+                columns(dproj_ref, pooled_ref, which, to),
+                columns(dproj_all, pooled_all, which, tab),
                 a_send.at[which, k], a_recv.at[which, k], to, rep,
             )
             copy.start()
             copies.append(copy)
         gathers.append(copies)
-    own = pltpu.make_async_copy(dproj_ref.at[tab], dproj_all.at[tab], own_sem.at[0])
-    own.start()
+    own = [
+        pltpu.make_async_copy(
+            dproj_ref.at[half, tab], dproj_all.at[half, tab], own_sem.at[half]
+        )
+        for half in range(2)
+    ]
+    for copy in own:
+        copy.start()
 
     for copy in loads[2:4]:
         copy.wait()
@@ -164,24 +173,8 @@
 
     lax.fori_loop(0, counts.shape[0] // step, count, 0)
 
-    buffers = [
-        (row_own, row_wire, row_sum),
-        (proj_own.at[0], proj_wire.at[0], proj_sum.at[0]),
-        (proj_own.at[1], proj_wire.at[1], proj_sum.at[1]),
-    ]
-
-    def send_all():
-        row_wire[0] = row_own[...].reshape(row_wire.shape[1:]).astype(BF16)
-        copies = []
-        for k in range(1, n_rep):
-            to = lax.rem(rep + k, n_rep)
-            slot = lax.rem(to, 2) * n_z + to // 2
-            copy = remote(
-                row_wire.at[0, slot], row_wire.at[1, k], c_send.at[k], c_recv.at[k], tab, to
-            )
-            copy.start()
-            copies.append(copy)
-        return copies
+    buffers = [(row_own.at[i], row_wire.at[i], row_sum.at[i]) for i in range(2)]
+    buffers += [(proj_own.at[i], proj_wire.at[i], proj_sum.at[i]) for i in range(2)]
 
     def send_pair(which):
         sums, wire, _ = buffers[which]
@@ -212,15 +205,15 @@
         for copy in line:
             copy.wait_recv()
         total = sums[y, z]
-        for k in range(1, n_rep if which == 0 else n_z):
-            total = total + (wire[1, k] if which == 0 else wire[3, k]).astype(F32)
-        if which == 0:
+        for k in range(1, n_z):
+            total = total + wire[3, k].astype(F32)
+        if which < 2:
             part = total.shape[0]
             coded, powers = encode(total)
             out[y, z, :part] = coded
             out[y, z, part:] = powers
         else:
-            first = (which - 1) * piece + (y * n_z + z) * total.shape[0]
+            first = (which - 2) * piece + (y * n_z + z) * total.shape[0]
             at = lax.broadcasted_iota(jnp.int32, total.shape, 0) + first
             out[y, z] = jnp.where(at < limit, total, 0.0).astype(BF16)
         block = out.at[y, z]
@@ -255,13 +248,14 @@
         total = None
         for k in range(n_tab):
             if k > 0:
-                gathers[1 + half][k - 1].wait_recv()
+                gathers[2 + half][k - 1].wait_recv()
             at = lax.rem(tab - k + n_tab, n_tab)
             block = (pooled_all if k > 0 else pooled_ref)[at, half * piece : (half + 1) * piece]
-            term = jnp.dot(block, dproj_all[at], preferred_element_type=F32)
+            both = jnp.concatenate([dproj_all[0, at], dproj_all[1, at]], axis=1)
+            term = jnp.dot(block, both, preferred_element_type=F32)
             total = term if total is None else total + term
         proj_own[half] = total.reshape(proj_own.shape[1:])
-        return send_pair(1 + half)
+        return send_pair(2 + half)
 
     for copy in loads[4:]:
         copy.wait()
@@ -279,9 +273,19 @@
     ]
 
     def table_rows(slot, half):
-        part = row_sum.shape[2] - SCALE_ROWS
+        part = row_sum.shape[3] - SCALE_ROWS
         total = jnp.concatenate(
-            [decode(row_sum[half, i, :part], row_sum[half, i, part:]) for i in range(n_z)], axis=0
+            [
+                jnp.concatenate(
+                    [
+                        decode(row_sum[i, half, at, :part], row_sum[i, half, at, part:])
+                        for at in range(n_z)
+                    ],
+                    axis=0,
+                )
+                for i in range(2)
+            ],
+            axis=1,
         )
         high = total.astype(BF16)
         low = (total - high.astype(F32)).astype(BF16)
@@ -291,36 +295,43 @@
         ) + lax.dot_general(low, weight, (((1,), (1,)), ((), ())), preferred_element_type=F32)
         stores[slot].start()
 
-    own.wait()
-    for copy in gathers[0]:
-        copy.wait_recv()
-    d_all = dproj_all[...].reshape(n_tab * n_samples, width)
-    row_own[...] = jnp.dot(counts[...], d_all, preferred_element_type=F32).reshape(row_own.shape)
-    line0 = send_all()
-    pair1 = project(0)
-    pair2 = project(1)
-    line1 = send_line(1, pair1)
-    line2 = send_line(2, pair2)
+    pairs = []
+    for half in range(2):
+        own[half].wait()
+        for copy in gathers[half]:
+            copy.wait_recv()
+        d_all = dproj_all[half].reshape(n_tab * n_samples, width)
+        row_part = jnp.dot(counts[...], d_all, preferred_element_type=F32)
+        row_own[half] = row_part.reshape(row_own.shape[1:])
+        pairs.append(send_pair(half))
+    line0 = send_line(0, pairs[0])
+    line1 = send_line(1, pairs[1])
+    pairs.append(project(0))
     sums0, last0 = send_sums(0, line0)
+    pairs.append(project(1))
     sums1, last1 = send_sums(1, line1)
+    line2 = send_line(2, pairs[2])
+    line3 = send_line(3, pairs[3])
     sums2, last2 = send_sums(2, line2)
     fwd0 = forward(0, sums0)
     fwd1 = forward(1, sums1)
+    table_rows(0, y)
+    sums3, last3 = send_sums(3, line3)
     fwd2 = forward(2, sums2)
-    table_rows(0, y)
-    for copy in [last0, *fwd0]:
+    for copy in [last0, last1, *fwd0, *fwd1]:
         copy.wait_recv()
     table_rows(1, 1 - y)
-    for half, copies in enumerate(([last1, *fwd1], [last2, *fwd2])):
+    fwd3 = forward(3, sums3)
+    for half, copies in enumerate(([last2, *fwd2], [last3, *fwd3])):
         for copy in copies:
             copy.wait_recv()
         stores[2 + half].start()
-    for copy in [
-        *gathers[0], *gathers[1], *gathers[2], pair1, pair2,
-        *line0, *line1, *line2, *sums0, *sums1, *sums2,
-        last0, last1, last2, *fwd0, *fwd1, *fwd2,
-    ]:
-        copy.wait_send()
+    for copies in [*gathers, pairs, line0, line1, line2, line3, sums0, sums1, sums2, sums3]:
+        for copy in copies:
+            copy.wait_send()
+    for copies in [[last0, last1, last2, last3], fwd0, fwd1, fwd2, fwd3]:
+        for copy in copies:
+            copy.wait_send()
     for copy in stores:
         copy.wait()
 
@@ -361,38 +372,36 @@
         in_specs=[hbm] * 6,
         out_specs=(hbm, hbm),
         scratch_shapes=[
-            pltpu.VMEM((2, n_z, part + SCALE_ROWS, width), jnp.int16),
+            pltpu.VMEM((2, 2, n_z, part + SCALE_ROWS, width // 2), jnp.int16),
             pltpu.VMEM((2, 2, n_z, proj_part, width), BF16),
             pltpu.VMEM((2, ROWS // 2, widest), F32),
             pltpu.VMEM((widest, width), BF16),
             pltpu.VMEM((n_samples, n_tab, width), BF16),
             pltpu.VMEM((n_samples, n_tab, widest), BF16),
-            pltpu.VMEM((n_tab, n_samples, width), BF16),
+            pltpu.VMEM((2, n_tab, n_samples, width // 2), BF16),
             pltpu.VMEM((n_tab, widest, n_samples), BF16),
             pltpu.VMEM((bag, group), jnp.int32),
             pltpu.VMEM((1, group), jnp.int32),
             pltpu.VMEM((widest, width), BF16),
             pltpu.SMEM((n_tab,), jnp.int32),
-            pltpu.VMEM((n_tab, n_samples, width), BF16),
+            pltpu.VMEM((2, n_tab, n_samples, width // 2), BF16),
             pltpu.VMEM((n_tab, widest, n_samples), BF16),
             pltpu.VMEM((ROWS, group), BF16),
-            pltpu.VMEM((2, n_z, part, width), F32),
-            pltpu.VMEM((2, n_rep, part, width), BF16),
+            pltpu.VMEM((2, 2, n_z, part, width // 2), F32),
+            pltpu.VMEM((2, 4, n_z, part, width // 2), BF16),
             pltpu.VMEM((2, 2, n_z, proj_part, width), F32),
             pltpu.VMEM((2, 4, n_z, proj_part, width), BF16),
             dma((6,)),
             dma((4,)),
-            dma((1,)),
-            dma((3, n_tab)),
-            dma((3, n_tab)),
-            dma((n_rep,)),
-            dma((n_rep,)),
-            dma((3,)),
-            dma((3,)),
-            dma((3, n_z)),
-            dma((3, n_z)),
-            dma((3, 2, n_z)),
-            dma((3, 2, n_z)),
+            dma((2,)),
+            dma((4, n_tab)),
+            dma((4, n_tab)),
+            dma((4,)),
+            dma((4,)),
+            dma((4, n_z)),
+            dma((4, n_z)),
+            dma((4, 2, n_z)),
+            dma((4, 2, n_z)),
         ],
         compiler_params=pltpu.CompilerParams(
             collective_id=0, has_side_effects=True, vmem_limit_bytes=60 << 20

time: 37.3 us -> 37.4 us (level)
  no operation moved by 1% of the time
where the time goes in v7:
time: 37.4 us; the launch traced here: 37.3 us
  Pallas kernels  36.6 us (98%)
  between operations  0.64 us (2%)
    pallas_call x1, Pallas kernels, fused(): pl.pallas_call(functools.partial(kernel, n_tab, n_rep), out_shape=(jax.Sh...  34.4 us
    pallas_call x1, Pallas kernels, fused(): pl.pallas_call(finish, out_shape=(jax.ShapeDtypeStruct(emb.shape, F32), j...  2.21 us

profile of v7, /device:TPU:0, one launch (start us, length us, event | category | flops | bytes accessed | tf_op | source)
XLA Modules:
  0.0 37.3 jit_solution(15105375657975427331)
XLA Ops:
  0.6 34.4 %shard_map.77 = (f32[2,256,512]{2,1,0:T(8,128)}, bf16[2,2,4,32,256]{4,3,2,1,0:T(8,128)(2,1)}) custom-call(bf16[128,4,256]{2,1,0:T(4,128)(2,1)} %bitcast.12, bf16[128,4,512]{2,1,0:T(4,128)(2,1)} %bitcast.11, s32[8,512]{1,0:T(8,128)} %bitcast.14, s32[1,512]{1,0:T(1,128)} %bitcast.15, bf16[4,512,256]{2,1,0:T(8,128)(2,1)} %weight_hbm.1, s32[4]{0:T(128)} %dims_hbm.1), custom_call_target="tpu_custom_call" | custom-call | tf_op jit(solution)/shard_map/pallas_call | solution.py:366
  35.1 2.2 %shard_map.78 = (f32[4,128,512]{2,1,0:T(8,128)}, f32[512,256]{1,0:T(8,128)}) custom-call(f32[4,128,512]{2,1,0:T(8,128)} %bitcast.10, bf16[512,256]{1,0:T(8,128)(2,1)} %bitcast.13), custom_call_target="tpu_custom_call" | custom-call | bytes 3145728 | tf_op jit(solution)/shard_map/pallas_call | solution.py:420

commit v8 on v6

--- a/solution.py
+++ b/solution.py
@@ -65,8 +65,6 @@
     own_sem,
     a_send,
     a_recv,
-    c_send,
-    c_recv,
     y_send,
     y_recv,
     z_send,
@@ -81,7 +79,6 @@
     z = rep // 2
     partner = rep + 1 - 2 * y
     n_samples, width = dproj_ref.shape[1], dproj_ref.shape[2]
-    piece = pooled_ref.shape[1] // 2
 
     loads = [
         pltpu.make_async_copy(src, dst, load_sem.at[i])
@@ -112,33 +109,28 @@
         pl.semaphore_signal(
             barrier, inc=1, device_id=(lax.rem(tab + k, n_tab), rep), device_id_type=MESH
         )
-    for k in range(1, n_rep):
+    for k in range(1, n_z):
         pl.semaphore_signal(
-            barrier, inc=1, device_id=(tab, lax.rem(rep + k, n_rep)), device_id_type=MESH
+            barrier, inc=1, device_id=(tab, lax.rem(rep + 2 * k, n_rep)), device_id_type=MESH
         )
+    pl.semaphore_signal(barrier, inc=1, device_id=(tab, partner), device_id_type=MESH)
     loads[0].wait()
     dproj_ref[...] = jnp.transpose(dproj_raw[...], (1, 0, 2))
-    pl.semaphore_wait(barrier, n_tab + n_rep - 2)
-
-    def columns(ref, at, which):
-        return ref.at[at] if which == 0 else ref.at[at, pl.ds((which - 1) * piece, piece)]
+    pl.semaphore_wait(barrier, n_tab - 1 + n_z)
 
     gathers = []
-    for which in range(3):
+    for which in range(2):
+        src, dst = (dproj_ref, dproj_all) if which == 0 else (pooled_ref, pooled_all)
         if which == 1:
             loads[1].wait()
             by_table = jnp.transpose(pooled_raw[...], (1, 0, 2))
-        if which > 0:
-            at = (which - 1) * piece
             for table in range(n_tab):
-                pooled_ref[table, at : at + piece] = by_table[table, :, at : at + piece].T
-        src, dst = (dproj_ref, dproj_all) if which == 0 else (pooled_ref, pooled_all)
+                pooled_ref[table] = by_table[table].T
         copies = []
         for k in range(1, n_tab):
             to = lax.rem(tab + k, n_tab)
             copy = remote(
-                columns(src, to, which), columns(dst, tab, which),
-                a_send.at[which, k], a_recv.at[which, k], to, rep,
+                src.at[to], dst.at[tab], a_send.at[which, k], a_recv.at[which, k], to, rep
             )
             copy.start()
             copies.append(copy)
@@ -164,24 +156,7 @@
 
     lax.fori_loop(0, counts.shape[0] // step, count, 0)
 
-    buffers = [
-        (row_own, row_wire, row_sum),
-        (proj_own.at[0], proj_wire.at[0], proj_sum.at[0]),
-        (proj_own.at[1], proj_wire.at[1], proj_sum.at[1]),
-    ]
-
-    def send_all():
-        row_wire[0] = row_own[...].reshape(row_wire.shape[1:]).astype(BF16)
-        copies = []
-        for k in range(1, n_rep):
-            to = lax.rem(rep + k, n_rep)
-            slot = lax.rem(to, 2) * n_z + to // 2
-            copy = remote(
-                row_wire.at[0, slot], row_wire.at[1, k], c_send.at[k], c_recv.at[k], tab, to
-            )
-            copy.start()
-            copies.append(copy)
-        return copies
+    buffers = [(row_own, row_wire, row_sum), (proj_own, proj_wire, proj_sum)]
 
     def send_pair(which):
         sums, wire, _ = buffers[which]
@@ -212,15 +187,15 @@
         for copy in line:
             copy.wait_recv()
         total = sums[y, z]
-        for k in range(1, n_rep if which == 0 else n_z):
-            total = total + (wire[1, k] if which == 0 else wire[3, k]).astype(F32)
+        for k in range(1, n_z):
+            total = total + wire[3, k].astype(F32)
         if which == 0:
             part = total.shape[0]
             coded, powers = encode(total)
             out[y, z, :part] = coded
             out[y, z, part:] = powers
         else:
-            first = (which - 1) * piece + (y * n_z + z) * total.shape[0]
+            first = (y * n_z + z) * total.shape[0]
             at = lax.broadcasted_iota(jnp.int32, total.shape, 0) + first
             out[y, z] = jnp.where(at < limit, total, 0.0).astype(BF16)
         block = out.at[y, z]
@@ -232,36 +207,27 @@
             )
             copy.start()
             copies.append(copy)
-        copy = remote(
-            block, block, g_send.at[which, 1, 0], g_recv.at[which, 1, 0], tab, partner
-        )
+        return copies
+
+    def forward(which, arriving):
+        for copy in arriving:
+            copy.wait_recv()
+        half = buffers[which][2].at[y]
+        copy = remote(half, half, g_send.at[which, 1, 0], g_recv.at[which, 1, 0], tab, partner)
         copy.start()
-        return copies, copy
-
-    def forward(which, arriving):
-        out = buffers[which][2]
-        copies = []
-        for k in range(1, n_z):
-            arriving[k - 1].wait_recv()
-            block = out.at[y, lax.rem(z - k + n_z, n_z)]
-            copy = remote(
-                block, block, g_send.at[which, 1, k], g_recv.at[which, 1, k], tab, partner
-            )
-            copy.start()
-            copies.append(copy)
-        return copies
-
-    def project(half):
+        return copy
+
+    def project():
         total = None
         for k in range(n_tab):
             if k > 0:
-                gathers[1 + half][k - 1].wait_recv()
+                gathers[1][k - 1].wait_recv()
             at = lax.rem(tab - k + n_tab, n_tab)
-            block = (pooled_all if k > 0 else pooled_ref)[at, half * piece : (half + 1) * piece]
+            block = (pooled_all if k > 0 else pooled_ref)[at]
             term = jnp.dot(block, dproj_all[at], preferred_element_type=F32)
             total = term if total is None else total + term
-        proj_own[half] = total.reshape(proj_own.shape[1:])
-        return send_pair(1 + half)
+        proj_own[...] = total.reshape(proj_own.shape)
+        return send_pair(1)
 
     for copy in loads[4:]:
         copy.wait()
@@ -273,8 +239,8 @@
         for i, (src, dst) in enumerate((
             (emb_buf.at[0], out_emb.at[y]),
             (emb_buf.at[1], out_emb.at[1 - y]),
-            (proj_sum.at[0], out_proj.at[0]),
-            (proj_sum.at[1], out_proj.at[1]),
+            (proj_sum.at[y], out_proj.at[y]),
+            (proj_sum.at[1 - y], out_proj.at[1 - y]),
         ))
     ]
 
@@ -296,30 +262,21 @@
         copy.wait_recv()
     d_all = dproj_all[...].reshape(n_tab * n_samples, width)
     row_own[...] = jnp.dot(counts[...], d_all, preferred_element_type=F32).reshape(row_own.shape)
-    line0 = send_all()
-    pair1 = project(0)
-    pair2 = project(1)
+    pair0 = send_pair(0)
+    line0 = send_line(0, pair0)
+    pair1 = project()
+    sums0 = send_sums(0, line0)
     line1 = send_line(1, pair1)
-    line2 = send_line(2, pair2)
-    sums0, last0 = send_sums(0, line0)
-    sums1, last1 = send_sums(1, line1)
-    sums2, last2 = send_sums(2, line2)
     fwd0 = forward(0, sums0)
+    table_rows(0, y)
+    sums1 = send_sums(1, line1)
+    fwd0.wait_recv()
+    table_rows(1, 1 - y)
     fwd1 = forward(1, sums1)
-    fwd2 = forward(2, sums2)
-    table_rows(0, y)
-    for copy in [last0, *fwd0]:
-        copy.wait_recv()
-    table_rows(1, 1 - y)
-    for half, copies in enumerate(([last1, *fwd1], [last2, *fwd2])):
-        for copy in copies:
-            copy.wait_recv()
-        stores[2 + half].start()
-    for copy in [
-        *gathers[0], *gathers[1], *gathers[2], pair1, pair2,
-        *line0, *line1, *line2, *sums0, *sums1, *sums2,
-        last0, last1, last2, *fwd0, *fwd1, *fwd2,
-    ]:
+    stores[2].start()
+    fwd1.wait_recv()
+    stores[3].start()
+    for copy in [*gathers[0], *gathers[1], pair0, pair1, *line0, *line1, *sums0, *sums1, fwd0, fwd1]:
         copy.wait_send()
     for copy in stores:
         copy.wait()
@@ -349,20 +306,20 @@
     n_samples, width, widest = d_proj.shape[1], d_proj.shape[3], pooled.shape[3]
     group, bag = bag_rows.shape[1], bag_rows.shape[3]
     n_z = n_rep // 2
-    part, proj_part = ROWS // n_rep, widest // 2 // n_rep
+    part, proj_part = ROWS // n_rep, widest // n_rep
     hbm = pl.BlockSpec(memory_space=pltpu.HBM)
     dma = pltpu.SemaphoreType.DMA
     emb, proj_grad = pl.pallas_call(
         functools.partial(kernel, n_tab, n_rep),
         out_shape=(
             jax.ShapeDtypeStruct((2, ROWS // 2, widest), F32),
-            jax.ShapeDtypeStruct((2, 2, n_z, proj_part, width), BF16),
+            jax.ShapeDtypeStruct((2, n_z, proj_part, width), BF16),
         ),
         in_specs=[hbm] * 6,
         out_specs=(hbm, hbm),
         scratch_shapes=[
             pltpu.VMEM((2, n_z, part + SCALE_ROWS, width), jnp.int16),
-            pltpu.VMEM((2, 2, n_z, proj_part, width), BF16),
+            pltpu.VMEM((2, n_z, proj_part, width), BF16),
             pltpu.VMEM((2, ROWS // 2, widest), F32),
             pltpu.VMEM((widest, width), BF16),
             pltpu.VMEM((n_samples, n_tab, width), BF16),
@@ -377,22 +334,20 @@
             pltpu.VMEM((n_tab, widest, n_samples), BF16),
             pltpu.VMEM((ROWS, group), BF16),
             pltpu.VMEM((2, n_z, part, width), F32),
-            pltpu.VMEM((2, n_rep, part, width), BF16),
-            pltpu.VMEM((2, 2, n_z, proj_part, width), F32),
-            pltpu.VMEM((2, 4, n_z, proj_part, width), BF16),
+            pltpu.VMEM((4, n_z, part, width), BF16),
+            pltpu.VMEM((2, n_z, proj_part, width), F32),
+            pltpu.VMEM((4, n_z, proj_part, width), BF16),
             dma((6,)),
             dma((4,)),
             dma((1,)),
-            dma((3, n_tab)),
-            dma((3, n_tab)),
-            dma((n_rep,)),
-            dma((n_rep,)),
-            dma((3,)),
-            dma((3,)),
-            dma((3, n_z)),
-            dma((3, n_z)),
-            dma((3, 2, n_z)),
-            dma((3, 2, n_z)),
+            dma((2, n_tab)),
+            dma((2, n_tab)),
+            dma((2,)),
+            dma((2,)),
+            dma((2, n_z)),
+            dma((2, n_z)),
+            dma((2, 2, n_z)),
+            dma((2, 2, n_z)),
         ],
         compiler_params=pltpu.CompilerParams(
             collective_id=0, has_side_effects=True, vmem_limit_bytes=60 << 20
@@ -474,7 +429,7 @@
     )
 
     def body(*args):
-        if n_rep % 2 == 0 and ROWS % (16 * n_rep) == 0 and args[2].shape[1] % (32 * n_rep) == 0:
+        if n_rep % 2 == 0 and ROWS % (16 * n_rep) == 0 and args[2].shape[1] % (16 * n_rep) == 0:
             return fused(n_tab, n_rep, *args)
         return general(*args)
 

time: 37.3 us -> 39.9 us (1.070)
  Pallas kernels: 36.5 us -> 39.1 us
    pallas_call x1, Pallas kernels: 34.3 us -> 36.9 us  [fused(): pl.pallas_call(functools.partial(kernel, n_tab, n_rep), out_shape=(jax.Sh...]
where the time goes in v8:
time: 39.9 us; the launch traced here: 39.8 us
  Pallas kernels  39.1 us (98%)
  between operations  0.64 us (2%)
    pallas_call x1, Pallas kernels, fused(): pl.pallas_call(functools.partial(kernel, n_tab, n_rep), out_shape=(jax.Sh...  36.9 us
    pallas_call x1, Pallas kernels, fused(): pl.pallas_call(finish, out_shape=(jax.ShapeDtypeStruct(emb.shape, F32), j...  2.21 us

profile of v8, /device:TPU:0, one launch (start us, length us, event | category | flops | bytes accessed | tf_op | source)
XLA Modules:
  0.0 39.8 jit_solution(17979294357394550488)
XLA Ops:
  0.6 36.9 %shard_map.77 = (f32[2,256,512]{2,1,0:T(8,128)}, bf16[2,4,64,256]{3,2,1,0:T(8,128)(2,1)}) custom-call(bf16[128,4,256]{2,1,0:T(4,128)(2,1)} %bitcast.12, bf16[128,4,512]{2,1,0:T(4,128)(2,1)} %bitcast.11, s32[8,512]{1,0:T(8,128)} %bitcast.14, s32[1,512]{1,0:T(1,128)} %bitcast.15, bf16[4,512,256]{2,1,0:T(8,128)(2,1)} %weight_hbm.1, s32[4]{0:T(128)} %dims_hbm.1), custom_call_target="tpu_custom_call" | custom-call | tf_op jit(solution)/shard_map/pallas_call | solution.py:312
  37.6 2.2 %shard_map.78 = (f32[4,128,512]{2,1,0:T(8,128)}, f32[512,256]{1,0:T(8,128)}) custom-call(f32[4,128,512]{2,1,0:T(8,128)} %bitcast.10, bf16[512,256]{1,0:T(8,128)(2,1)} %bitcast.13), custom_call_target="tpu_custom_call" | custom-call | bytes 3145728 | tf_op jit(solution)/shard_map/pallas_call | solution.py:366

commit v9 on v6

--- a/solution.py
+++ b/solution.py
@@ -65,8 +65,6 @@
     own_sem,
     a_send,
     a_recv,
-    c_send,
-    c_recv,
     y_send,
     y_recv,
     z_send,
@@ -97,6 +95,13 @@
     for copy in loads:
         copy.start()
 
+    n_x = n_tab // 2
+    offsets = [(dx, dc) for dx in range(1, n_x) for dc in range(2)] + [(0, 1)]
+    x, core = tab // 2, lax.rem(tab, 2)
+
+    def owner(dx, dc):
+        return 2 * lax.rem(x + dx + n_x, n_x) + lax.rem(core + dc, 2)
+
     def remote(src, dst, send, recv, tab_to, rep_to):
         return pltpu.make_async_remote_copy(
             src_ref=src,
@@ -112,13 +117,14 @@
         pl.semaphore_signal(
             barrier, inc=1, device_id=(lax.rem(tab + k, n_tab), rep), device_id_type=MESH
         )
-    for k in range(1, n_rep):
+    for k in range(1, n_z):
         pl.semaphore_signal(
-            barrier, inc=1, device_id=(tab, lax.rem(rep + k, n_rep)), device_id_type=MESH
+            barrier, inc=1, device_id=(tab, lax.rem(rep + 2 * k, n_rep)), device_id_type=MESH
         )
+    pl.semaphore_signal(barrier, inc=1, device_id=(tab, partner), device_id_type=MESH)
     loads[0].wait()
     dproj_ref[...] = jnp.transpose(dproj_raw[...], (1, 0, 2))
-    pl.semaphore_wait(barrier, n_tab + n_rep - 2)
+    pl.semaphore_wait(barrier, n_tab - 1 + n_z)
 
     def columns(ref, at, which):
         return ref.at[at] if which == 0 else ref.at[at, pl.ds((which - 1) * piece, piece)]
@@ -134,8 +140,8 @@
                 pooled_ref[table, at : at + piece] = by_table[table, :, at : at + piece].T
         src, dst = (dproj_ref, dproj_all) if which == 0 else (pooled_ref, pooled_all)
         copies = []
-        for k in range(1, n_tab):
-            to = lax.rem(tab + k, n_tab)
+        for k, offset in enumerate(offsets):
+            to = owner(*offset)
             copy = remote(
                 columns(src, to, which), columns(dst, tab, which),
                 a_send.at[which, k], a_recv.at[which, k], to, rep,
@@ -169,19 +175,6 @@
         (proj_own.at[0], proj_wire.at[0], proj_sum.at[0]),
         (proj_own.at[1], proj_wire.at[1], proj_sum.at[1]),
     ]
-
-    def send_all():
-        row_wire[0] = row_own[...].reshape(row_wire.shape[1:]).astype(BF16)
-        copies = []
-        for k in range(1, n_rep):
-            to = lax.rem(rep + k, n_rep)
-            slot = lax.rem(to, 2) * n_z + to // 2
-            copy = remote(
-                row_wire.at[0, slot], row_wire.at[1, k], c_send.at[k], c_recv.at[k], tab, to
-            )
-            copy.start()
-            copies.append(copy)
-        return copies
 
     def send_pair(which):
         sums, wire, _ = buffers[which]
@@ -212,8 +205,8 @@
         for copy in line:
             copy.wait_recv()
         total = sums[y, z]
-        for k in range(1, n_rep if which == 0 else n_z):
-            total = total + (wire[1, k] if which == 0 else wire[3, k]).astype(F32)
+        for k in range(1, n_z):
+            total = total + wire[3, k].astype(F32)
         if which == 0:
             part = total.shape[0]
             coded, powers = encode(total)
@@ -253,11 +246,12 @@
 
     def project(half):
         total = None
-        for k in range(n_tab):
-            if k > 0:
-                gathers[1 + half][k - 1].wait_recv()
-            at = lax.rem(tab - k + n_tab, n_tab)
-            block = (pooled_all if k > 0 else pooled_ref)[at, half * piece : (half + 1) * piece]
+        for k in [None, *reversed(range(n_tab - 1))]:
+            at = tab
+            if k is not None:
+                gathers[1 + half][k].wait_recv()
+                at = owner(-offsets[k][0], offsets[k][1])
+            block = (pooled_ref if k is None else pooled_all)[at, half * piece : (half + 1) * piece]
             term = jnp.dot(block, dproj_all[at], preferred_element_type=F32)
             total = term if total is None else total + term
         proj_own[half] = total.reshape(proj_own.shape[1:])
@@ -296,8 +290,9 @@
         copy.wait_recv()
     d_all = dproj_all[...].reshape(n_tab * n_samples, width)
     row_own[...] = jnp.dot(counts[...], d_all, preferred_element_type=F32).reshape(row_own.shape)
-    line0 = send_all()
+    pair0 = send_pair(0)
     pair1 = project(0)
+    line0 = send_line(0, pair0)
     pair2 = project(1)
     line1 = send_line(1, pair1)
     line2 = send_line(2, pair2)
@@ -316,7 +311,7 @@
             copy.wait_recv()
         stores[2 + half].start()
     for copy in [
-        *gathers[0], *gathers[1], *gathers[2], pair1, pair2,
+        *gathers[0], *gathers[1], *gathers[2], pair0, pair1, pair2,
         *line0, *line1, *line2, *sums0, *sums1, *sums2,
         last0, last1, last2, *fwd0, *fwd1, *fwd2,
     ]:
@@ -377,7 +372,7 @@
             pltpu.VMEM((n_tab, widest, n_samples), BF16),
             pltpu.VMEM((ROWS, group), BF16),
             pltpu.VMEM((2, n_z, part, width), F32),
-            pltpu.VMEM((2, n_rep, part, width), BF16),
+            pltpu.VMEM((4, n_z, part, width), BF16),
             pltpu.VMEM((2, 2, n_z, proj_part, width), F32),
             pltpu.VMEM((2, 4, n_z, proj_part, width), BF16),
             dma((6,)),
@@ -385,8 +380,6 @@
             dma((1,)),
             dma((3, n_tab)),
             dma((3, n_tab)),
-            dma((n_rep,)),
-            dma((n_rep,)),
             dma((3,)),
             dma((3,)),
             dma((3, n_z)),

time: 37.3 us -> 36.3 us (0.973)
  Pallas kernels: 36.5 us -> 35.5 us
    pallas_call x1, Pallas kernels: 34.3 us -> 33.3 us  [fused(): pl.pallas_call(functools.partial(kernel, n_tab, n_rep), out_shape=(jax.Sh...]
where the time goes in v9:
time: 36.3 us; the launch traced here: 36.1 us
  Pallas kernels  35.5 us (98%)
  between operations  0.64 us (2%)
    pallas_call x1, Pallas kernels, fused(): pl.pallas_call(functools.partial(kernel, n_tab, n_rep), out_shape=(jax.Sh...  33.3 us
    pallas_call x1, Pallas kernels, fused(): pl.pallas_call(finish, out_shape=(jax.ShapeDtypeStruct(emb.shape, F32), j...  2.21 us

profile of v9, /device:TPU:0, one launch (start us, length us, event | category | flops | bytes accessed | tf_op | source)
XLA Modules:
  0.0 36.1 jit_solution(17106109931384948471)
XLA Ops:
  0.6 33.3 %shard_map.77 = (f32[2,256,512]{2,1,0:T(8,128)}, bf16[2,2,4,32,256]{4,3,2,1,0:T(8,128)(2,1)}) custom-call(bf16[128,4,256]{2,1,0:T(4,128)(2,1)} %bitcast.12, bf16[128,4,512]{2,1,0:T(4,128)(2,1)} %bitcast.11, s32[8,512]{1,0:T(8,128)} %bitcast.14, s32[1,512]{1,0:T(1,128)} %bitcast.15, bf16[4,512,256]{2,1,0:T(8,128)(2,1)} %weight_hbm.1, s32[4]{0:T(128)} %dims_hbm.1), custom_call_target="tpu_custom_call" | custom-call | tf_op jit(solution)/shard_map/pallas_call | solution.py:350
  33.9 2.2 %shard_map.78 = (f32[4,128,512]{2,1,0:T(8,128)}, f32[512,256]{1,0:T(8,128)}) custom-call(f32[4,128,512]{2,1,0:T(8,128)} %bitcast.10, bf16[512,256]{1,0:T(8,128)(2,1)} %bitcast.13), custom_call_target="tpu_custom_call" | custom-call | bytes 3145728 | tf_op jit(solution)/shard_map/pallas_call | solution.py:404
